TPU v7x, 128 devices: a whole 4x4x4 slice. The times are simulated.
128 devices in a mesh: expert: 16 (over z, y), fsdp: 8 (over x, core).
Axes of the slice: x: 4, y: 4, z: 4, core: 2. Of those that a mesh axis runs over, the one named last changes fastest.
Arguments:
- tokens: bfloat16 [2, 8, 2048, 1024], P(None, 'fsdp', 'expert'), may hold values from -6 to 6
- cotangent: bfloat16 [2, 8, 2048, 1024], P(None, 'fsdp', 'expert'), may hold values from -6 to 6
- doc_lengths: int32 [2, 8, 3], P(None, 'fsdp'), may hold values from 1 to 2046, as said below
- routes: int32 [2, 8, 2048, 2], P(None, 'fsdp', 'expert'), may hold values from 0 to 15, all different within a row
- order: int32 [2, 8, 16, 256], P(None, 'fsdp', 'expert'), may hold values from 0 to 255, each once within a row
- gain_attn: bfloat16 [1024], P(('expert', 'fsdp')), may hold values from 0.5 to 1.5
- w_query: bfloat16 [1024, 1024], P(('expert', 'fsdp')), may hold values from -0.1875 to 0.1875
- w_key: bfloat16 [1024, 1024], P(('expert', 'fsdp')), may hold values from -0.1875 to 0.1875
- w_value: bfloat16 [1024, 1024], P(('expert', 'fsdp')), may hold values from -0.1875 to 0.1875
- w_out: bfloat16 [1024, 1024], P(('expert', 'fsdp')), may hold values from -1 to 1
- rel_table: bfloat16 [512], P(('expert', 'fsdp')), may hold values from -3 to 3
- gain_moe: bfloat16 [1024], P(('expert', 'fsdp')), may hold values from 0.5 to 1.5
- w_router: bfloat16 [1024, 16], P(('expert', 'fsdp')), may hold values from -0.125 to 0.125
- w_gate: bfloat16 [16, 1024, 2816], P('expert', None, 'fsdp'), may hold values from -0.1875 to 0.1875
- w_up: bfloat16 [16, 1024, 2816], P('expert', None, 'fsdp'), may hold values from -0.1875 to 0.1875
- w_down: bfloat16 [16, 2816, 1024], P('expert', 'fsdp'), may hold values from -0.15625 to 0.15625
Outputs:
- output: bfloat16 [2, 8, 2048, 1024], P(None, 'fsdp', 'expert')
- input_grad: bfloat16 [2, 8, 2048, 1024], P(None, 'fsdp', 'expert')
- grad_gain_attn: float32 [1024], P(('expert', 'fsdp'))
- grad_query: float32 [1024, 1024], P(('expert', 'fsdp'))
- grad_key: float32 [1024, 1024], P(('expert', 'fsdp'))
- grad_value: float32 [1024, 1024], P(('expert', 'fsdp'))
- grad_out: float32 [1024, 1024], P(('expert', 'fsdp'))
- grad_table: float32 [512], P(('expert', 'fsdp'))
- grad_gain_moe: float32 [1024], P(('expert', 'fsdp'))
- grad_router: float32 [1024, 16], P(('expert', 'fsdp'))
- grad_gate: float32 [16, 1024, 2816], P('expert', None, 'fsdp')
- grad_up: float32 [16, 1024, 2816], P('expert', None, 'fsdp')
- grad_down: float32 [16, 2816, 1024], P('expert', 'fsdp')
Inputs may be any that keep to these rules, and one draw needn't show every extreme that they name: `doc_lengths`: in each sequence the first and last documents are shorter than 128 tokens and the middle one holds the rest; in some sequence the first and last documents hold one token each. The two routes of a token differ. Each block's slots in an order of precedence, each number once.
All inputs are finite; a program needn't handle non-finite values.
Results may differ from a plain program's by a relative error of at most 0.035.
Values may be sent and summed in bfloat16 or wider, within the bound.
A program may use at most 256 MiB of HBM per device.

v0:
```python
import jax
import jax.numpy as jnp
from jax import lax
from jax.experimental import pallas as pl
from jax.experimental.pallas import tpu as pltpu
from jax.sharding import PartitionSpec as P

H = 16
HD = 64
NB = 32
D = 1024
FF = 2816
WINDOW = 1024
EXPERTS = 16
CAP = 20
TS = 128
FSDP = 8
SHARD = FF // FSDP
TOK = 2 * TS
BUF = EXPERTS * 2 * CAP
SEQ = EXPERTS * TS
EPS = 1e-06
MASKED = -1e30
EDGES = tuple(range(1, 17)) + (19, 21, 24, 27, 31, 35, 40, 46, 52, 59, 67, 77, 87, 99, 113)
GELU_C = 0.7978845608028654
BF = jnp.bfloat16
F32 = jnp.float32
VMEM_LIMIT = 58 * 1024 * 1024


def nn(left, right):
    return lax.dot_general(left, right, (((1,), (0,)), ((), ())), preferred_element_type=F32)


def nt(left, right):
    return lax.dot_general(left, right, (((1,), (1,)), ((), ())), preferred_element_type=F32)


def tn(left, right):
    return lax.dot_general(left, right, (((0,), (0,)), ((), ())), preferred_element_type=F32)


def halves(value):
    high = value.astype(BF)
    return high, (value - high.astype(F32)).astype(BF)


def call(kernel, out_shape, *args, scratch=(), in_specs=None, out_specs=None, collective_id=None):
    return pl.pallas_call(
        kernel,
        out_shape=out_shape,
        in_specs=in_specs or [pl.BlockSpec(memory_space=pltpu.VMEM)] * len(args),
        out_specs=out_specs or jax.tree.map(lambda _: pl.BlockSpec(memory_space=pltpu.VMEM), out_shape),
        scratch_shapes=list(scratch),
        compiler_params=pltpu.CompilerParams(
            vmem_limit_bytes=VMEM_LIMIT,
            collective_id=collective_id,
            has_side_effects=collective_id is not None,
        ),
    )(*args)


def shape(dims, dtype):
    return jax.ShapeDtypeStruct(dims, dtype)


def lane_half(dims):
    return lax.broadcasted_iota(jnp.int32, dims, 1) % 128 < HD


def pack_pair(first, second):
    left = lane_half(first.shape)
    return (
        jnp.where(left, first, pltpu.roll(second, HD, 1)).astype(BF),
        jnp.where(left, pltpu.roll(first, HD, 1), second).astype(BF),
    )


MESH = pl.DeviceIdType.MESH
HALF = D // 2
WIDE = 4 * HALF + 128
GATHER_PARTS = ((pl.ds(0, 896), "xzy"), (pl.ds(896, 896), "xyz"), (pl.ds(1792, 384), "zyx"))
REDUCE_PARTS = ((pl.ds(0, 768), "zyx"), (pl.ds(768, 768), "yzx"), (pl.ds(1536, 640), "xyz"))


def coords():
    e, f = lax.axis_index("expert"), lax.axis_index("fsdp")
    return lax.div(e, 4), lax.rem(e, 4), lax.div(f, 2), lax.rem(f, 2)


def device(z, y, x, c):
    return (z * 4 + y, x * 2 + c)


def ring(at, step):
    return lax.rem(at + step, 4)


def greet(peers):
    barrier = pltpu.get_barrier_semaphore()
    for peer in peers:
        pl.semaphore_signal(barrier, inc=1, device_id=peer, device_id_type=MESH)
    pl.semaphore_wait(barrier, len(peers))


class Copies:
    def __init__(self, send_sem, recv_sem):
        self.send_sem, self.recv_sem, self.started = send_sem, recv_sem, []

    def go(self, src, dst, peer):
        at = len(self.started)
        copy = pltpu.make_async_remote_copy(
            src_ref=src,
            dst_ref=dst,
            send_sem=self.send_sem.at[at],
            recv_sem=self.recv_sem.at[at],
            device_id=peer,
            device_id_type=MESH,
        )
        copy.start()
        self.started.append(copy)
        return copy

    def drain(self):
        for copy in self.started:
            copy.wait_send()


def plane_peers():
    e, f = lax.axis_index("expert"), lax.axis_index("fsdp")
    return [(lax.rem(e + k, EXPERTS), f) for k in range(1, EXPERTS)]


class Exchange:
    def __init__(self, held, landed, send_sem, recv_sem, rows=None):
        self.held, self.landed, self.send_sem, self.recv_sem = held, landed, send_sem, recv_sem
        self.rows = rows or pl.ds(0, held.shape[1])
        self.me, self.f = lax.axis_index("expert"), lax.axis_index("fsdp")

    def copy(self, to):
        step = lax.rem(to - self.me + EXPERTS, EXPERTS)
        return pltpu.make_async_remote_copy(
            src_ref=self.held.at[to, self.rows],
            dst_ref=self.landed.at[self.me, self.rows],
            send_sem=self.send_sem.at[step],
            recv_sem=self.recv_sem.at[step],
            device_id=(to, self.f),
            device_id_type=MESH,
        )

    def others(self, act):
        def body(k, carry):
            act(self.copy(lax.rem(self.me + k, EXPERTS)))
            return carry

        lax.fori_loop(1, EXPERTS, body, 0)

    def keep(self):
        self.landed[self.me, self.rows] = self.held[self.me, self.rows]

    def push(self, to):
        @pl.when(to != self.me)
        def _():
            self.copy(to).start()

        @pl.when(to == self.me)
        def _():
            self.keep()

    def start(self):
        self.others(lambda copy: copy.start())
        self.keep()

    def arrive(self):
        self.others(lambda copy: copy.wait_recv())

    def drain(self):
        self.others(lambda copy: copy.wait_send())


def spread(value):
    half = D // 2
    parts = [value[:, at : at + half].reshape(EXPERTS, 2 * CAP, half) for at in (0, half)]
    return jnp.concatenate(parts, axis=1).astype(BF)


def unspread(ref, into):
    half = D // 2
    value = ref[...].astype(F32)
    for side in range(2):
        part = value[:, side * 2 * CAP : (side + 1) * 2 * CAP, :].reshape(BUF, half)
        into[:, side * half : (side + 1) * half] = part.astype(BF)


class Place:
    def __init__(self):
        self.z, self.y, self.x, self.c = coords()
        self.at = {"z": self.z, "y": self.y, "x": self.x}
        self.twin = device(self.z, self.y, self.x, 1 - self.c)

    def moved(self, axis, step):
        return {**self.at, axis: ring(self.at[axis], step)}

    def peer(self, axis, step):
        to = self.moved(axis, step)
        return device(to["z"], to["y"], to["x"], self.c)

    def peers(self, axes):
        return [self.peer(axis, k) for axis in axes for k in (1, 2, 3)]


class Gather:
    def __init__(self, place, box, copies, lanes, order):
        self.place, self.box, self.copies, self.lanes, self.order = place, box, copies, lanes, order
        self.phases, self.forwards = [], []

    def region(self, known, at):
        spots = tuple(slice(None) if axis in known else at[axis] for axis in "zyx")
        return self.box.at[spots + (self.place.c, slice(None), self.lanes)]

    def start(self, phase):
        axis, known = self.order[phase], self.order[:phase]
        here = self.region(known, self.place.at)
        self.phases.append([self.copies.go(here, here, self.place.peer(axis, k)) for k in (1, 2, 3)])

    def forward_own(self):
        here = self.region("", self.place.at)
        self.forwards.append(self.copies.go(here, here, self.place.twin))

    def forward(self, phase, k):
        axis, known = self.order[phase], self.order[:phase]
        got = self.region(known, self.place.moved(axis, 4 - k))
        self.forwards.append(self.copies.go(got, got, self.place.twin))

    def arrive(self, phase, forward=False):
        for k, copy in enumerate(self.phases[phase]):
            copy.wait_recv()
            if forward:
                self.forward(phase, k + 1)

    def forward_all(self, phase):
        for k in (1, 2, 3):
            self.forward(phase, k)

    def finish(self):
        for copy in self.forwards:
            copy.wait_recv()


class Reduce:
    def __init__(self, place, copies, order, first, held, landed):
        self.place, self.copies, self.order = place, copies, order
        self.sources, self.landed, self.started = [first] + list(held), landed, [[], [], []]

    def pick(self, phase, spot):
        left = [axis for axis in "zyx" if axis in self.order[phase:]]
        return tuple(spot if axis == self.order[phase] else slice(None) for axis in left)

    def send(self, phase, k):
        axis = self.order[phase]
        src, lanes = self.sources[phase]
        spots = self.pick(phase, ring(self.place.at[axis], k))
        src = src.at[spots + (slice(None), lanes)]
        self.started[phase].append(
            self.copies.go(src, self.landed[phase].at[k - 1], self.place.peer(axis, k))
        )

    def start(self, phase):
        for k in (1, 2, 3):
            self.send(phase, k)

    def total(self, phase):
        for copy in self.started[phase]:
            copy.wait_recv()
        src, lanes = self.sources[phase]
        spots = self.pick(phase, self.place.at[self.order[phase]])
        value = src[spots + (slice(None), lanes)].astype(F32)
        for k in range(3):
            value = value + self.landed[phase][k].astype(F32)
        if phase < 2:
            nxt, width = self.sources[phase + 1]
            nxt[...] = value.astype(BF)
        return value


def reduce_scratch(width):
    return [
        pltpu.VMEM((4, 4, 16, width), BF), pltpu.VMEM((4, 16, width), BF),
        pltpu.VMEM((3, 4, 4, 16, width), BF), pltpu.VMEM((3, 4, 16, width), BF), pltpu.VMEM((3, 16, width), BF),
    ]


def folded(value):
    return jnp.concatenate([value[:, : D // 2], value[:, D // 2 :]], axis=0)


def unfolded(value):
    return jnp.concatenate([value[:8], value[8:]], axis=1)


def fold_rows(value):
    half = D // 2
    return jnp.concatenate(
        [value[:, at : at + half].reshape(32, 8, half) for at in (0, half)], axis=1
    )


def unfold_into(ref, plane, value):
    half = D // 2
    rows = slice(plane * 256, plane * 256 + 256)
    ref[rows, :half] = value[:, :8, :].reshape(256, half).astype(BF)
    ref[rows, half:] = value[:, 8:, :].reshape(256, half).astype(BF)


def lane_pick():
    col = lax.broadcasted_iota(jnp.int32, (128, D), 1)
    return (lax.rem(col, 8) == lax.broadcasted_iota(jnp.int32, (128, D), 0)).astype(BF)


def own_columns():
    col = lax.broadcasted_iota(jnp.int32, (128, D), 1)
    low = lax.broadcasted_iota(jnp.int32, (128, D), 0) * 8
    return (col >= low) & (col < low + 8)


def by_device(row):
    high, low = halves(jnp.where(own_columns(), row, 0.0))
    pick = lane_pick()
    return nt(high, pick) + nt(low, pick)


def pick_row(values, row):
    at = lax.broadcasted_iota(jnp.int32, values.shape, values.ndim - 2)
    return jnp.sum(jnp.where(at == row, values, 0.0), axis=-2)


def gather_kernel(
    x_ref, wq_ref, wk_ref, wv_ref, wo_ref, small_ref,
    normed_ref, land_ref, wq_out, wk_out, wv_out, wo_out, wr_out, gain_out, tab_out,
    box, out_ref, send_sem, recv_sem, trade_send, trade_recv,
):
    place = Place()
    z, y, x, c = place.z, place.y, place.x, place.c
    for k, w_ref in enumerate((wq_ref, wk_ref, wv_ref, wo_ref)):
        box[z, y, x, c, :, k * HALF : (k + 1) * HALF] = folded(w_ref[...].astype(F32)).astype(BF)
    box[z, y, x, c, :, 4 * HALF :] = small_ref[...]
    greet(plane_peers() + place.peers("x") + [place.twin])
    copies = Copies(send_sem, recv_sem)
    trade = Exchange(out_ref, land_ref, trade_send, trade_recv)
    both = [Gather(place, box, copies, lanes, order) for lanes, order in GATHER_PARTS]
    for part in both:
        part.start(0)
    for part in both:
        part.forward_own()
    tokens = x_ref[...].astype(F32)
    unit = tokens * lax.rsqrt(jnp.mean(tokens * tokens, axis=-1, keepdims=True) + EPS)
    for phase in (0, 1):
        for part in both:
            part.arrive(phase)
            part.start(phase + 1)
        for part in both:
            part.forward_all(phase)
    for part in both:
        part.arrive(2, forward=True)
    for part in both:
        part.finish()

    def unfold(k, w_out):
        for plane in range(4):
            value = box[plane, :, :, :, :, k * HALF : (k + 1) * HALF].reshape(32, 16, HALF)
            unfold_into(w_out, plane, value.astype(F32))

    for k, w_out in enumerate((wq_out, wk_out, wv_out)):
        unfold(k, w_out)
    small = box[:, :, :, :, :, 4 * HALF :].reshape(128, 16, 128).astype(F32)
    lane = lax.broadcasted_iota(jnp.int32, (D, 128), 1)
    wr_out[...] = jnp.where(lane < EXPERTS, small[:, :8, :].reshape(D, 128), 0.0).astype(BF)
    pick, mine = lane_pick(), own_columns()
    gains = [
        jnp.sum(jnp.where(mine, nn(pick_row(small[:, 8:, :], row).astype(BF), pick), 0.0), axis=0, keepdims=True)
        for row in range(2)
    ]
    gain_out[...] = jnp.concatenate(gains + [jnp.zeros((6, D), F32)], axis=0)
    near = box[z, y, :, :, :, 4 * HALF :].reshape(8, 16, 128).astype(F32)
    tab_out[...] = pick_row(near, 10)

    normed = (unit * gains[0]).astype(BF)
    normed_ref[...] = normed
    for k in (1, 2, 3, 0):
        part = ring(z, k)
        for which, w_ref in enumerate((wq_out, wk_out, wv_out)):
            res = nn(normed, w_ref[:, pl.ds(pl.multiple_of(part * 256, 256), 256)])
            for pair in range(2):
                head = part * 4 + pair * 2
                cols = slice(pair * 128, pair * 128 + 128)
                first, second = pack_pair(res[:TS, cols], res[TS:, cols])
                out_ref[head, which * TS : (which + 1) * TS, :] = first
                out_ref[head + 1, which * TS : (which + 1) * TS, :] = second
        for j in (1, 2, 3, 0):
            if k or j:
                trade.copy(part * 4 + ring(y, j)).start()
            else:
                trade.keep()
    unfold(3, wo_out)
    trade.arrive()
    trade.drain()
    copies.drain()


def attn_setup(len_ref, tab_ref, recv_ref, kext, qext, bias):
    rows = lax.broadcasted_iota(jnp.int32, (SEQ, 128), 0)
    lanes = lax.broadcasted_iota(jnp.int32, (SEQ, 128), 1)
    end1 = [len_ref[m, 0] for m in range(2)]
    end2 = [len_ref[m, 0] + len_ref[m, 1] for m in range(2)]
    kfeat = jnp.where(lanes == 4, 1.0, 0.0)
    for m in range(2):
        kfeat = jnp.where((lanes == 2 * m) & (rows < end1[m]), 1.0, kfeat)
        kfeat = jnp.where((lanes == 2 * m + 1) & (rows < end2[m]), 1.0, kfeat)
    kext[:, 128:] = kfeat.astype(BF)
    for i in range(EXPERTS):
        kext[i * TS : (i + 1) * TS, :128] = recv_ref[i, TS : 2 * TS, :]
    left = lane_half((TS, 128))
    row_in = lax.broadcasted_iota(jnp.int32, (TS, 128), 0)
    lane_in = lax.broadcasted_iota(jnp.int32, (TS, 128), 1)
    for i in range(EXPERTS):
        q2 = recv_ref[i, 0:TS, :].astype(F32) * (HD**-0.5)
        pos = row_in + i * TS
        for m in range(2):
            keep = left if m == 0 else jnp.logical_not(left)
            qext[i, m * TS : (m + 1) * TS, :128] = jnp.where(keep, q2, 0.0).astype(BF)
            feat = jnp.where((lane_in == 2 * m) & (pos >= end1[m]), MASKED, 0.0)
            feat = jnp.where((lane_in == 2 * m + 1) & (pos >= end2[m]), MASKED, feat)
            qext[i, m * TS : (m + 1) * TS, 128:] = feat.astype(BF)
    for block in range(12):
        dist = 1024 - block * TS + lane_in - row_in
        if block in (7, 8):
            value = jnp.broadcast_to(tab_ref[0:1, 0:1], (TS, 128))
            for bucket, edge in enumerate(EDGES):
                b = bucket + 1
                value = jnp.where(dist >= edge, tab_ref[b // 4 : b // 4 + 1, b % 4 : b % 4 + 1], value)
        else:
            value = jnp.broadcast_to(tab_ref[7:8, 3:4], (TS, 128))
        value = jnp.where((dist >= 0) & (dist < WINDOW), value, MASKED)
        bias[block * TS : (block + 1) * TS, :128] = value
        bias[block * TS : (block + 1) * TS, 128:] = value


def eye(size):
    return (
        lax.broadcasted_iota(jnp.int32, (size, size), 0)
        == lax.broadcasted_iota(jnp.int32, (size, size), 1)
    ).astype(BF)


def loop(strip, low, high, count):
    def body(i, carry):
        strip(i, count, i - 8 if count == 9 else 0)
        return carry

    lax.fori_loop(low, high, body, 0)


def span(block, count):
    return pl.ds(pl.multiple_of(block * TS, TS), count * TS)


def attn_fwd_kernel(
    len_ref, tab_ref, recv_ref, land_ref, lse_ref, kext, qext, bias, vt, out_ref, send_sem, recv_sem
):
    greet(plane_peers())
    trade = Exchange(out_ref, land_ref, send_sem, recv_sem)
    attn_setup(len_ref, tab_ref, recv_ref, kext, qext, bias)
    unit = eye(TS)
    for i in range(EXPERTS):
        vt[:, i * TS : (i + 1) * TS] = nt(unit, recv_ref[i, 2 * TS : 3 * TS, :]).astype(BF)

    def strip(i, count, first):
        s = nt(kext[span(first, count), :], qext[i]) + bias[span(first - i + 8, count), :]
        top = jnp.max(s, axis=0, keepdims=True)
        p = jnp.exp(s - top)
        total = jnp.sum(p, axis=0, keepdims=True)
        res = nn(vt[:, span(first, count)], p.astype(BF)) / total
        both = jnp.concatenate([res[:HD, :TS], res[HD:, TS:]], axis=0)
        out_ref[i] = both.T.astype(BF)
        lse_ref[i] = jnp.broadcast_to(top + jnp.log(total), (8, TOK))
        trade.push(i)

    loop(strip, 0, 4, 4)
    loop(strip, 4, 8, 8)
    loop(strip, 8, 16, 9)
    trade.arrive()
    trade.drain()


def attn_bwd_kernel(
    len_ref, tab_ref, recv_ref, dout_ref, lse_ref, land_ref, tab_out_ref,
    kext, qext, bias, ktext, dk, dv, near, far, out_ref, *sems,
):
    greet(plane_peers())
    trade_q = Exchange(out_ref, land_ref, sems[0], sems[1], pl.ds(0, TS))
    trade_kv = Exchange(out_ref, land_ref, sems[2], sems[3], pl.ds(TS, 2 * TS))
    attn_setup(len_ref, tab_ref, recv_ref, kext, qext, bias)
    unit = eye(256)
    for i in range(EXPERTS):
        ktext[:, i * TS : (i + 1) * TS] = nt(unit, kext[i * TS : (i + 1) * TS, :])[:144].astype(BF)
    dk[...] = jnp.zeros_like(dk)
    dv[...] = jnp.zeros_like(dv)
    near[...] = jnp.zeros_like(near)
    far[...] = jnp.zeros_like(far)
    left = lane_half((TS, 128))

    def strip(i, count, first):
        q = qext[i]
        s = nt(kext[span(first, count), :], q) + bias[span(first - i + 8, count), :]
        p = jnp.exp(s - lse_ref[i][0:1])
        do2 = dout_ref[i]
        zero = jnp.zeros_like(do2)
        do = jnp.concatenate([jnp.where(left, do2, zero), jnp.where(left, zero, do2)], axis=0)
        if count == 9:
            v = recv_ref[pl.ds(first, count), 2 * TS : 3 * TS, :].reshape(count * TS, 128)
        else:
            v = recv_ref[0:count, 2 * TS : 3 * TS, :].reshape(count * TS, 128)
        dp = nt(v, do)
        inner = jnp.sum(p * dp, axis=0, keepdims=True)
        ds = (p * (dp - inner)).astype(BF)
        dv[span(first, count), :] += nn(p.astype(BF), do)
        dk[span(first, count), :] += nn(ds, q[:, :128])
        dqt = nn(ktext[:, span(first, count)], ds)
        both = jnp.concatenate([dqt[:HD, :TS], dqt[HD : 2 * HD, TS:]], axis=0) * (HD**-0.5)
        out_ref[i, 0:TS, :] = both.T.astype(BF)
        trade_q.push(i)
        far[...] += dqt[128:136]
        if count == 9:
            near[...] += ds[7 * TS :].astype(F32)
        else:
            nearby.append(ds)

    nearby = []

    def finish(block):
        out_ref[block, TS : 2 * TS, :] = dk[span(block, 1), :].astype(BF)
        out_ref[block, 2 * TS :, :] = dv[span(block, 1), :].astype(BF)
        trade_kv.push(block)

    def sweep(low, high, count):
        def body(i, carry):
            nearby.clear()
            first = i - 8 if count == 9 else 0
            strip(i, count, first)
            if count == 9:
                finish(first)
            else:
                ds = nearby[0]
                for block in range(count):
                    value = ds[block * TS : (block + 1) * TS].astype(F32)

                    @pl.when(i == block)
                    def _(value=value):
                        near[TS:] += value

                    @pl.when(i == block + 1)
                    def _(value=value):
                        near[:TS] += value

            return carry

        lax.fori_loop(low, high, body, 0)

    sweep(0, 4, 4)
    sweep(4, 8, 8)
    sweep(8, 16, 9)

    def rest(block, carry):
        finish(block)
        return carry

    lax.fori_loop(8, EXPERTS, rest, 0)
    grads = near[:, :TS] + near[:, TS:]
    dist = (
        TS
        + lax.broadcasted_iota(jnp.int32, (TOK, TS), 1)
        - lax.broadcasted_iota(jnp.int32, (TOK, TS), 0)
    )
    total = jnp.sum(far[4:5, :])
    lane = lax.broadcasted_iota(jnp.int32, (8, 128), 1)
    lane = jnp.where(lane < 4, lane + 4 * lax.broadcasted_iota(jnp.int32, (8, 128), 0), NB)
    res = jnp.zeros((8, 128), F32)
    lows = (0,) + EDGES
    seen = 0.0
    for b in range(NB - 1):
        part = jnp.sum(jnp.where((dist >= lows[b]) & (dist < lows[b + 1]), grads, 0.0))
        seen = seen + part
        res = jnp.where(lane == b, part, res)
    res = jnp.where(lane == NB - 1, total - seen, res)
    tab_out_ref[...] = res
    for trade in (trade_q, trade_kv):
        trade.arrive()
        trade.drain()


def row_expert():
    row = lax.broadcasted_iota(jnp.int32, (BUF, 128), 0)
    lane = lax.broadcasted_iota(jnp.int32, (BUF, 128), 1) * (2 * CAP)
    return (row >= lane) & (row < lane + 2 * CAP)


def unpack_heads(recv_ref, lo, emit):
    for pair in range(H // 2):
        one = recv_ref[2 * pair, lo : lo + TS, :].astype(F32)
        two = recv_ref[2 * pair + 1, lo : lo + TS, :].astype(F32)
        first, second = pack_pair(one, two)
        emit(pair, first, second)


def slot_share(place, share_e, own):
    high, low = halves(share_e)
    return jnp.sum(jnp.where(own, nn(place, high) + nn(place, low), 0.0), axis=1, keepdims=True)


FFC = 2 * SHARD
STEPS = FF // FFC


def moe_kernel(
    recv_ref, x_ref, wo_ref, gain_ref, wr_ref, mask_ref, place_ref, dy_ref, w_ref,
    att_ref, hidden_ref, mixed_ref, share_ref, back_out, back_row, grads_ref,
    w_buf, hold_a, hold_b, land_a, land_b, rows, slots, act, first, second, acc, stage,
    w_sem, stage_sem, *sems,
):
    def load(step):
        slot = lax.rem(step, 2)
        return pltpu.make_async_copy(w_ref.at[pl.ds(step * 2, 2)], w_buf.at[slot], w_sem.at[slot])

    load(0).start()
    load(1).start()
    greet(plane_peers())
    to_rows = Exchange(hold_a, land_a, sems[0], sems[1])
    to_slots = Exchange(hold_b, land_b, sems[2], sems[3])
    from_out = Exchange(hold_a, back_out, sems[4], sems[5])
    from_row = Exchange(hold_b, back_row, sems[6], sems[7])

    def emit(pair, one, two):
        att_ref[0:TS, pair * 128 : pair * 128 + 128] = one
        att_ref[TS:, pair * 128 : pair * 128 + 128] = two

    unpack_heads(recv_ref, 0, emit)
    hidden = x_ref[...].astype(F32) + nn(att_ref[...], wo_ref[...])
    hidden_ref[...] = hidden
    factor = lax.rsqrt(jnp.mean(hidden * hidden, axis=-1, keepdims=True) + EPS)
    mixed = (hidden * factor * gain_ref[1:2, :]).astype(BF)
    mixed_ref[...] = mixed
    place = place_ref[...]
    hold_a[...] = spread(nn(place, mixed))
    to_rows.start()
    picked = mask_ref[...] > 0
    logits = jnp.where(picked, nn(mixed, wr_ref[...]), MASKED)
    weight = jnp.exp(logits - jnp.max(logits, axis=1, keepdims=True))
    share = weight / jnp.sum(weight, axis=1, keepdims=True)
    share_ref[...] = share
    hold_b[...] = spread(slot_share(place, share, row_expert()) * nn(place, dy_ref[...]))

    to_rows.arrive()
    to_slots.start()
    unspread(land_a, rows)
    acc[...] = jnp.zeros_like(acc)

    def weights(step):
        w = w_buf[lax.rem(step, 2)]
        return [w[:, k * SHARD : (k + 1) * SHARD, :].reshape(FFC, D) for k in range(3)]

    def forward(step, carry):
        load(step).wait()
        gate_w, up_w, down_w = weights(step)
        gate = nt(rows[...], gate_w)
        up = nt(rows[...], up_w)
        square = gate * gate
        tanh = jnp.tanh(GELU_C * gate * (1.0 + 0.044715 * square))
        half_up = 0.5 * (1.0 + tanh)
        gelu = gate * half_up
        slope = half_up + 0.5 * gate * (1.0 - tanh * tanh) * (
            GELU_C * (1.0 + 3 * 0.044715 * square)
        )
        acted = (gelu * up).astype(BF)
        act[step] = acted
        first[step] = (up * slope).astype(BF)
        second[step] = gelu.astype(BF)
        acc[...] += nn(acted, down_w)

        @pl.when(step < STEPS - 2)
        def _():
            load(step + 2).start()

        return carry

    lax.fori_loop(0, STEPS, forward, 0)
    to_rows.drain()
    hold_a[...] = spread(acc[...])
    from_out.start()
    to_slots.arrive()
    unspread(land_b, slots)
    acc[...] = jnp.zeros_like(acc)

    def backward(at, carry):
        step = STEPS - 1 - at

        @pl.when(at >= 2)
        def _():
            load(step).wait()

        gate_w, up_w, down_w = weights(step)
        act_grad = nt(slots[...], down_w).astype(BF).astype(F32)
        gate_grad = (act_grad * first[step].astype(F32)).astype(BF)
        up_grad = (act_grad * second[step].astype(F32)).astype(BF)
        first[step] = gate_grad
        second[step] = up_grad
        acc[...] += nn(gate_grad, gate_w) + nn(up_grad, up_w)

        @pl.when(at < 2)
        def _():
            load(step - 2).start()

        return carry

    lax.fori_loop(0, STEPS, backward, 0)
    to_slots.drain()
    hold_b[...] = spread(acc[...])
    from_row.start()

    def store(step, which):
        return pltpu.make_async_copy(
            stage.at[which],
            grads_ref.at[pl.ds(step * 2, 2), pl.ds(which * SHARD, SHARD)],
            stage_sem.at[which],
        )

    def weight_grads(step, carry):
        for which, (left, right) in enumerate(((first, rows), (second, rows), (act, slots))):
            value = tn(left[step], right[...]).astype(BF).reshape(2, SHARD, D)

            @pl.when(step > 0)
            def _(which=which):
                store(step - 1, which).wait()

            stage[which] = value
            store(step, which).start()
        return carry

    lax.fori_loop(0, STEPS, weight_grads, 0)
    for which in range(3):
        store(STEPS - 1, which).wait()
    from_out.arrive()
    from_row.arrive()
    from_out.drain()
    from_row.drain()


def back_kernel(
    out_ref, row_ref, place_ref, place_t_ref, dy_ref, hidden_ref, mixed_ref, share_ref, wr_ref, gain_ref, wo_ref,
    result_ref, hgrad_ref, branch_ref, land_ref, router_ref, gain_out_ref,
    send_ref, outs, rows, send_sem, recv_sem,
):
    greet(plane_peers())
    z, y, _, _ = coords()
    trade = Exchange(send_ref, land_ref, send_sem, recv_sem)
    unspread(out_ref, outs)
    unspread(row_ref, rows)
    place = place_ref[...]
    place_t = place_t_ref[...]
    own = row_expert()
    dy = dy_ref[...]
    returned = outs[...]
    dots = jnp.sum(nn(place, dy) * returned.astype(F32), axis=1, keepdims=True)
    high, low = halves(jnp.where(own, dots, 0.0))
    share = share_ref[...]
    share_grad = nn(place_t, high) + nn(place_t, low)
    inner = jnp.sum(share * share_grad, axis=1, keepdims=True)
    lg_high, lg_low = halves(share * (share_grad - inner))
    wr = wr_ref[...]
    mixed_grad = nn(place_t, rows[...]) + (nt(lg_high, wr) + nt(lg_low, wr))
    hidden = hidden_ref[...]
    factor = lax.rsqrt(jnp.mean(hidden * hidden, axis=-1, keepdims=True) + EPS)
    unit = hidden * factor
    gain_out_ref[...] = jnp.broadcast_to(jnp.sum(mixed_grad * unit, axis=0, keepdims=True), (8, D))
    scaled = mixed_grad * gain_ref[1:2, :]
    hgrad = dy.astype(F32) + factor * (
        scaled - unit * jnp.mean(scaled * unit, axis=-1, keepdims=True)
    )
    hgrad_ref[...] = hgrad
    branch = hgrad.astype(BF)
    branch_ref[...] = branch
    for k in (1, 2, 3, 0):
        part = ring(z, k)
        res = nt(branch, wo_ref[pl.ds(pl.multiple_of(part * 256, 256), 256), :])
        for pair in range(2):
            head = part * 4 + pair * 2
            cols = slice(pair * 128, pair * 128 + 128)
            one, two = pack_pair(res[:TS, cols], res[TS:, cols])
            send_ref[head] = one
            send_ref[head + 1] = two
        for j in (1, 2, 3, 0):
            if k or j:
                trade.copy(part * 4 + ring(y, j)).start()
            else:
                trade.keep()
    mixed = mixed_ref[...]
    router_ref[...] = tn(mixed, lg_high) + tn(mixed, lg_low)
    scale_high, scale_low = halves(
        place_t.astype(F32) * slot_share(place, share, own).T
    )
    moe = nn(scale_high, returned) + nn(scale_low, returned)
    result_ref[...] = (hidden + moe).astype(BF)
    trade.arrive()
    trade.drain()


def final_kernel(
    recv_ref, normed_ref, x_ref, gains_ref, hgrad_ref, wq_ref, wk_ref, wv_ref,
    att_ref, branch_ref, router_ref, moe_gain_ref, table_ref, igrad_ref, sum_ref,
    flat_q, flat_k, flat_v, box, from_twin, *rest,
):
    place = Place()
    z, y, c = place.z, place.y, place.c
    greet(place.peers("xyz") + [place.twin])
    copies = Copies(rest[15], rest[16])
    parts = [
        Reduce(
            place, copies, order, (from_twin, lanes),
            [(bufs[0], pl.ds(0, lanes.size)), (bufs[1], pl.ds(0, lanes.size))], bufs[2:],
        )
        for (lanes, order), bufs in zip(REDUCE_PARTS, (rest[0:5], rest[5:10], rest[10:15]))
    ]
    flats = (flat_q, flat_k, flat_v)
    for which, flat in enumerate(flats):

        def emit(pair, first, second):
            flat[0:TS, pair * 128 : pair * 128 + 128] = first
            flat[TS:, pair * 128 : pair * 128 + 128] = second

        unpack_heads(recv_ref, which * TS, emit)

    total = nt(flat_q[...], wq_ref[...]) + nt(flat_k[...], wk_ref[...]) + nt(flat_v[...], wv_ref[...])
    tokens = x_ref[...].astype(F32)
    factor = lax.rsqrt(jnp.mean(tokens * tokens, axis=-1, keepdims=True) + EPS)
    unit = tokens * factor

    at = lax.broadcasted_iota(jnp.int32, (128, 8, 128), 1)
    gains = [by_device(row) for row in (jnp.sum(total * unit, axis=0, keepdims=True), moe_gain_ref[0:1, :])]
    lower = jnp.where(at == 0, gains[0][:, None, :], 0.0) + jnp.where(at == 1, gains[1][:, None, :], 0.0)
    extra = jnp.concatenate([router_ref[...].reshape(128, 8, 128), lower], axis=1)
    box[:, :, :, :, :, 4 * HALF :] = extra.astype(BF).reshape(4, 4, 4, 2, 16, 128)
    at = lax.broadcasted_iota(jnp.int32, (8, 16, 128), 1)
    here = box[z, y, :, :, :, 4 * HALF :].reshape(8, 16, 128).astype(F32)
    here = here + jnp.where(at == 10, table_ref[...][:, None, :], 0.0)
    box[z, y, :, :, :, 4 * HALF :] = here.astype(BF).reshape(4, 2, 16, 128)

    planes = [ring(z, k) for k in (1, 2, 3, 0)]
    to_twin = []
    for plane in planes:
        cols = pl.ds(pl.multiple_of(plane * 256, 256), 256)
        for which, (left, flat) in enumerate(
            ((normed_ref, flat_q), (normed_ref, flat_k), (normed_ref, flat_v), (att_ref, branch_ref))
        ):
            value = fold_rows(tn(left[:, cols], flat[...])).astype(BF)
            box[plane, :, :, :, :, which * HALF : (which + 1) * HALF] = value.reshape(4, 4, 2, 16, HALF)
        to_twin.append(copies.go(box.at[plane, :, :, 1 - c], from_twin.at[plane], place.twin))

    for k, plane in enumerate(planes):
        to_twin[k].wait_recv()
        both = box[plane, :, :, c].astype(F32) + from_twin[plane].astype(F32)
        from_twin[plane] = both.astype(BF)
        if k < 3:
            parts[0].send(0, k + 1)
    parts[1].start(0)
    parts[2].start(0)
    scaled = total * gains_ref[0:1, :]
    igrad_ref[...] = (
        hgrad_ref[...]
        + factor * (scaled - unit * jnp.mean(scaled * unit, axis=-1, keepdims=True))
    ).astype(BF)
    for phase in range(2):
        for part in parts:
            part.total(phase)
            part.start(phase + 1)
    value = jnp.concatenate([part.total(2) for part in parts], axis=1)
    for which in range(4):
        sum_ref[which * 8 : which * 8 + 8, :] = unfolded(value[:, which * HALF : (which + 1) * HALF])
    sum_ref[32:48, 0:128] = value[:, 4 * HALF :]
    copies.drain()


def placement(routes, order):
    micro = routes.shape[0]
    slots = routes.reshape(micro, 2 * TS)
    rank_of = order.reshape(micro, 2 * TS)
    same = slots[:, :, None] == slots[:, None, :]
    earlier = rank_of[:, None, :] < rank_of[:, :, None]
    rank = jnp.sum((same & earlier).astype(jnp.int32), axis=2)
    base = slots * (2 * CAP) + jnp.arange(micro, dtype=jnp.int32)[:, None] * CAP
    target = jnp.where(rank < CAP, base + rank, BUF).reshape(micro * TS, 2)
    rows = jnp.arange(BUF, dtype=jnp.int32)
    place = (rows[:, None] == target[None, :, 0]) | (rows[:, None] == target[None, :, 1])
    place_t = (rows[None, :] == target[:, 0:1]) | (rows[None, :] == target[:, 1:2])
    return place.astype(BF), place_t.astype(BF)


def on_device(
    tokens, cotangent, doc_lengths, routes, order, gain_attn, w_query, w_key, w_value, w_out,
    rel_table, gain_moe, w_router, w_gate, w_up, w_down,
):
    expert_shard = jnp.concatenate([w_gate[0].T, w_up[0].T, w_down[0]], axis=0)
    expert_w = lax.all_gather(expert_shard, "fsdp", axis=0, tiled=False)

    def padded(value):
        return jnp.pad(value, ((0, 0), (0, 128 - value.shape[1])))

    small = jnp.concatenate(
        [padded(v) for v in (w_router, gain_attn[None], gain_moe[None], rel_table[None])]
        + [jnp.zeros((5, 128), BF)],
        axis=0,
    )
    place, place_t = placement(routes[:, 0], order[:, 0, 0])
    lanes = jnp.arange(128, dtype=jnp.int32)
    route_rows = routes.reshape(TOK, 2)
    picked = (
        (route_rows[:, 0:1] == lanes) | (route_rows[:, 1:2] == lanes)
    ).astype(F32)
    x = tokens.reshape(TOK, D)
    dy = cotangent.reshape(TOK, D)
    lengths = doc_lengths[:, 0]

    normed, heads, wq, wk, wv, wo, wr, gains, table = call(
        gather_kernel,
        (
            shape((TOK, D), BF), shape((H, 3 * TS, 128), BF), shape((D, D), BF), shape((D, D), BF),
            shape((D, D), BF), shape((D, D), BF), shape((D, 128), BF), shape((8, D), F32), shape((8, 128), F32),
        ),
        x, w_query, w_key, w_value, w_out, small,
        scratch=[
            pltpu.VMEM((4, 4, 4, 2, 16, WIDE), BF),
            pltpu.VMEM((H, 3 * TS, 128), BF),
            pltpu.SemaphoreType.DMA((57,)),
            pltpu.SemaphoreType.DMA((57,)),
            pltpu.SemaphoreType.DMA((EXPERTS,)),
            pltpu.SemaphoreType.DMA((EXPERTS,)),
        ],
        collective_id=1,
    )
    smem = pl.BlockSpec(memory_space=pltpu.SMEM)
    vmem = pl.BlockSpec(memory_space=pltpu.VMEM)
    attn_scratch = [
        pltpu.VMEM((SEQ, 256), BF),
        pltpu.VMEM((EXPERTS, TOK, 256), BF),
        pltpu.VMEM((12 * TS, TOK), F32),
    ]
    att_back, lse = call(
        attn_fwd_kernel,
        (shape((EXPERTS, TS, 128), BF), shape((EXPERTS, 8, TOK), F32)),
        lengths, table, heads,
        in_specs=[smem, vmem, vmem],
        scratch=attn_scratch
        + [pltpu.VMEM((128, SEQ), BF), pltpu.VMEM((EXPERTS, TS, 128), BF)]
        + [pltpu.SemaphoreType.DMA((EXPERTS,))] * 2,
        collective_id=5,
    )
    chunk = (EXPERTS, 4 * CAP, D // 2)
    anywhere = pl.BlockSpec(memory_space=pl.ANY)
    att, hidden, mixed, share, outs, row_grads, expert_grads = call(
        moe_kernel,
        (
            shape((TOK, D), BF), shape((TOK, D), F32), shape((TOK, D), BF), shape((TOK, 128), F32),
            shape(chunk, BF), shape(chunk, BF), shape((FSDP, 3 * SHARD, D), BF),
        ),
        att_back, x, wo, gains, wr, picked, place, dy, expert_w,
        in_specs=[vmem] * 8 + [anywhere],
        out_specs=(vmem,) * 6 + (anywhere,),
        scratch=[
            pltpu.VMEM((2, 2, 3 * SHARD, D), BF),
            pltpu.VMEM(chunk, BF), pltpu.VMEM(chunk, BF), pltpu.VMEM(chunk, BF), pltpu.VMEM(chunk, BF),
            pltpu.VMEM((BUF, D), BF), pltpu.VMEM((BUF, D), BF),
            pltpu.VMEM((STEPS, BUF, FFC), BF), pltpu.VMEM((STEPS, BUF, FFC), BF), pltpu.VMEM((STEPS, BUF, FFC), BF),
            pltpu.VMEM((BUF, D), F32),
            pltpu.VMEM((3, 2, SHARD, D), BF),
            pltpu.SemaphoreType.DMA((2,)), pltpu.SemaphoreType.DMA((3,)),
        ]
        + [pltpu.SemaphoreType.DMA((EXPERTS,))] * 8,
        collective_id=3,
    )
    expert_sum = lax.psum_scatter(
        expert_grads.reshape(FSDP * 3 * SHARD, D), "fsdp", scatter_dimension=0, tiled=True
    )
    result, hgrad, branch, head_grads, router_grad, moe_gain_grad = call(
        back_kernel,
        (
            shape((TOK, D), BF), shape((TOK, D), F32), shape((TOK, D), BF),
            shape((H, TS, 128), BF), shape((D, 128), F32), shape((8, D), F32),
        ),
        outs, row_grads, place, place_t, dy, hidden, mixed, share, wr, gains, wo,
        scratch=[
            pltpu.VMEM((H, TS, 128), BF), pltpu.VMEM((BUF, D), BF), pltpu.VMEM((BUF, D), BF),
            pltpu.SemaphoreType.DMA((EXPERTS,)), pltpu.SemaphoreType.DMA((EXPERTS,)),
        ],
        collective_id=4,
    )
    token_grads, table_grad = call(
        attn_bwd_kernel,
        (shape((EXPERTS, 3 * TS, 128), BF), shape((8, 128), F32)),
        lengths, table, heads, head_grads, lse,
        in_specs=[smem] + [vmem] * 4,
        scratch=attn_scratch
        + [
            pltpu.VMEM((144, SEQ), BF),
            pltpu.VMEM((SEQ, 128), F32),
            pltpu.VMEM((SEQ, 128), F32),
            pltpu.VMEM((2 * TS, TOK), F32),
            pltpu.VMEM((8, TOK), F32),
            pltpu.VMEM((EXPERTS, 3 * TS, 128), BF),
        ]
        + [pltpu.SemaphoreType.DMA((EXPERTS,))] * 4,
        collective_id=6,
    )
    input_grad, sums = call(
        final_kernel,
        (shape((TOK, D), BF), shape((48, D), F32)),
        token_grads, normed, x, gains, hgrad, wq, wk, wv, att, branch, router_grad, moe_gain_grad, table_grad,
        scratch=[
            pltpu.VMEM((TOK, D), BF), pltpu.VMEM((TOK, D), BF), pltpu.VMEM((TOK, D), BF),
            pltpu.VMEM((4, 4, 4, 2, 16, WIDE), BF),
            pltpu.VMEM((4, 4, 4, 16, WIDE), BF),
        ]
        + [buf for lanes, _ in REDUCE_PARTS for buf in reduce_scratch(lanes.size)]
        + [pltpu.SemaphoreType.DMA((31,))] * 2,
        collective_id=2,
    )
    return (
        result.reshape(tokens.shape),
        input_grad.reshape(tokens.shape),
        sums[40, :8],
        sums[0:8],
        sums[8:16],
        sums[16:24],
        sums[24:32],
        sums[42, :4],
        sums[41, :8],
        sums[32:40, :EXPERTS],
        expert_sum[:SHARD].astype(F32).T[None],
        expert_sum[SHARD : 2 * SHARD].astype(F32).T[None],
        expert_sum[2 * SHARD :].astype(F32)[None],
    )


def solution(mesh):
    row = P(None, "fsdp", "expert", None)
    flat = P(("expert", "fsdp"))
    matrix = P(("expert", "fsdp"), None)
    columns = P("expert", None, "fsdp")
    deep = P("expert", "fsdp", None)
    return jax.shard_map(
        on_device,
        mesh=mesh,
        in_specs=(
            row, row, P(None, "fsdp", None), row, row, flat, matrix, matrix, matrix, matrix,
            flat, flat, matrix, columns, columns, deep,
        ),
        out_specs=(
            row, row, flat, matrix, matrix, matrix, matrix, flat, flat, matrix, columns, columns, deep,
        ),
        check_vma=False,
    )
```

profile of v0, /device:TPU:1, one launch (start us, length us, event | category | flops | bytes accessed | tf_op | source)
XLA Modules:
  0.0 342.3 jit_solution(4745429518864971708)
XLA Ops:
  7.2 3.1 pad_maximum_fusion
  10.4 0.6 copy-done.3
  11.0 0.1 copy.36
  11.2 0.1 eq.110
  11.4 0.3 convert_reduce_fusion
  11.7 0.1 reduce_sum.12
  11.8 0.1 copy.37
  11.9 1.2 concatenate.6.small_ref
  13.1 78.0 %shard_map.255 = (bf16[256,1024]{1,0:T(8,128)(2,1)}, bf16[16,384,128]{2,1,0:T(8,128)(2,1)}, bf16[1024,1024]{1,0:T(8,128)(2,1)}, bf16[1024,1024]{1,0:T(8,128)(2,1...) custom-call(bf16[256,1024]{1,0:T(8,128)(2,1)} %bitcast.57, ...), custom_call_target="tpu_custom_call" | custom-call | tf_op jit(solution)/shard_map/pallas_call | solution.py:49
  91.1 21.2 %shard_map.256 = (bf16[16,128,128]{2,1,0:T(8,128)(2,1)}, f32[16,8,256]{2,1,0:T(8,128)}) custom-call(s32[2,3]{1,0:T(2,128)} %bitcast.75, f32[8,128]{1,0:T(8,128)} %get-tuple-element.41.tab_ref, bf16[16,384,128]{2,1,0:T(8,128)(2,1)} %get-tuple-element.42.recv_ref), custom_call_target="tpu_custom_call" | custom-call | tf_op jit(solution)/shard_map/pallas_call | solution.py:49
  112.4 0.8 fusion.6.mask_ref
  113.2 0.9 fusion.2.place_ref
  114.0 90.8 %shard_map.257 = (bf16[256,1024]{1,0:T(8,128)(2,1)}, f32[256,1024]{1,0:T(8,128)}, bf16[256,1024]{1,0:T(8,128)(2,1)}, f32[256,128]{1,0:T(8,128)}, bf16[16,80,512]...) custom-call(bf16[16,128,128]{2,1,0:T(8,128)(2,1)} %get-tuple-element.43.recv_ref, ...), custom_call_target="tpu_custom_call" | custom-call | tf_op jit(solution)/shard_map/pallas_call | solution.py:49
  204.9 0.9 fusion.4.place_t_ref
  205.8 21.3 %shard_map.258 = (bf16[256,1024]{1,0:T(8,128)(2,1)}, f32[256,1024]{1,0:T(8,128)}, bf16[256,1024]{1,0:T(8,128)(2,1)}, bf16[16,128,128]{2,1,0:T(8,128)(2,1)}, f32[1024,128]{1,0:T(8,128)}, /*index=5*/f32[8,1024]{1,0:T(8,128)}) custom-call(bf16[16,80,512]{2,1,0:T(8,128)(2,1)} %get-tuple-element.47.out_ref, bf16[16,80,512]{2,1,0:T(8,128)(2,1)} %get-tuple-element.48.row_ref, ...), custom_call_target="tpu_custom_call" | custom-call | tf_op jit(solution)/shard_map/pallas_call | solution.py:49
  227.1 38.4 %shard_map.259 = (bf16[16,384,128]{2,1,0:T(8,128)(2,1)}, f32[8,128]{1,0:T(8,128)}) custom-call(s32[2,3]{1,0:T(2,128)} %bitcast.76, f32[8,128]{1,0:T(8,128)} %get-tuple-element.41.tab_ref, bf16[16,384,128]{2,1,0:T(8,128)(2,1)} %get-tuple-element.42.recv_ref, bf16[16,128,128]{2,1,0:T(8,128)(2,1)} %get-tuple-element.53.dout_ref, ...), custom_call_target="tpu_custom_call" | custom-call | tf_op jit(solution)/shard_map/pallas_call | solution.py:49
  265.5 59.1 %shard_map.260 = (bf16[256,1024]{1,0:T(8,128)(2,1)}, f32[48,1024]{1,0:T(8,128)}) custom-call(bf16[16,384,128]{2,1,0:T(8,128)(2,1)} %get-tuple-element.55.recv_ref, bf16[256,1024]{1,0:T(8,128)(2,1)} %get-tuple-element.56.normed_ref, bf16[256,1024]{1,0:T(8,128)(2,1)} %bitcast.59, f32[8,1024]{1,0:T(8,128)} %get-tuple-element.45.gain_ref.gains_ref, ...), custom_call_target="tpu_custom_call" | custom-call | tf_op jit(solution)/shard_map/pallas_call | solution.py:49
  324.6 1.3 slice.58
  325.9 1.2 slice_bitcast_fusion.2
  327.1 1.3 slice_bitcast_fusion.1
  328.3 1.5 fusion.7
  329.8 3.8 %fusion = (f32[1,352,1024]{2,1,0:T(8,128)}, f32[1,1024,352]{1,2,0:T(8,128)}, f32[1,1024,352]{1,2,0:T(8,128)}) fusion(bf16[1056,1024]{1,0:T(8,128)(2,1)} %reduce-scatter.2.cloned.1.call-done), kind=kLoop, calls=%fused_computation.4 | loop fusion | flops 1081344 | bytes 6488064 | tf_op jit(solution)/shard_map/broadcast_in_dim | solution.py:1047
  333.7 0.8 copy.46
  334.5 0.8 copy.47
  (32 shorter events, 0.3 us)
Async XLA Ops:
  7.2 106.9 %all-gather.3.cloned.1.call-start = ((), (), s32[]{:S(2)}) async-start(), calls=%async_computation.2 | async-start | bytes 19464192 | tf_op jit(solution)/shard_map/all_gather | solution.py:911
  10.3 0.7 copy-start.3
  10.3 0.7 copy-start.5
  10.3 0.7 copy-start.6
  10.3 0.7 copy-start.7
  10.3 0.7 copy-start.2
  10.3 1.0 copy-start.4
  10.4 319.5 %reduce-scatter.2.cloned.1.call-start = ((), (), s32[]{:S(2)}) async-start(), calls=%async_computation.1 | async-start | bytes 19464192 | tf_op jit(solution)/shard_map/reduce_scatter | solution.py:988
  329.8 3.9 %copy-start = (bf16[256,1024]{1,0:T(8,128)(2,1)S(1)}, bf16[256,1024]{1,0:T(8,128)(2,1)}, u32[]{:S(2)}) copy-start(bf16[256,1024]{1,0:T(8,128)(2,1)} %get-tuple-element.52) | copy-start | bytes 1572868
  329.8 4.7 %copy-start.1 = (bf16[256,1024]{1,0:T(8,128)(2,1)S(1)}, bf16[256,1024]{1,0:T(8,128)(2,1)}, u32[]{:S(2)}) copy-start(bf16[256,1024]{1,0:T(8,128)(2,1)} %get-tuple-element.66) | copy-start | bytes 1572868
Sparse Core Ops, SparseCore 0:
  10.5 99.1 all-gather.2
  205.0 109.7 reduce-scatter.1
where the time goes:
time: 347 us; the launch traced here: 342 us
  Pallas kernels  309 us (89%)
  between operations  14.4 us (4%)
  other arithmetic  9.77 us (3%)
  local copies, waits for them, and re-layouts  9.17 us (3%)
    pallas_call x6, Pallas kernels, call(): pl.pallas_call(kernel, out_shape=out_shape, in_specs=in_specs or [pl.Bloc...  309 us
  transfers between devices with their start and end apart: 2, of which 0 were waited for; matrix products, arithmetic and copies ran while one was open for 3% of the time, Pallas kernels for 64%

commit v1 on v0

--- a/solution.py
+++ b/solution.py
@@ -79,8 +79,15 @@
 MESH = pl.DeviceIdType.MESH
 HALF = D // 2
 WIDE = 4 * HALF + 128
-GATHER_PARTS = ((pl.ds(0, 896), "xzy"), (pl.ds(896, 896), "xyz"), (pl.ds(1792, 384), "zyx"))
-REDUCE_PARTS = ((pl.ds(0, 768), "zyx"), (pl.ds(768, 768), "yzx"), (pl.ds(1536, 640), "xyz"))
+SMALL, OUT = 3 * HALF, 3 * HALF + 128
+GATHER_PARTS = ((pl.ds(0, 896), "xzy"), (pl.ds(896, 768), "xyz"))
+LATE_PARTS = ((pl.ds(OUT, 256), "xzy"), (pl.ds(OUT + 256, 256), "xyz"))
+REDUCE_PARTS = (
+    (pl.ds(0, 1024), "zyx"), (pl.ds(1024, 640), "yzx"), (pl.ds(1664, 384), "xyz"), (pl.ds(2048, 128), "yzx"),
+)
+EARLY = 32
+MAIN = pl.ds(0, 4 * HALF)
+REST = pl.ds(4 * HALF, 128)
 
 
 def coords():
@@ -184,9 +191,9 @@
     return jnp.concatenate(parts, axis=1).astype(BF)
 
 
-def unspread(ref, into):
+def unspread(into, *refs):
     half = D // 2
-    value = ref[...].astype(F32)
+    value = jnp.concatenate([ref[...].astype(F32) for ref in refs], axis=1)
     for side in range(2):
         part = value[:, side * 2 * CAP : (side + 1) * 2 * CAP, :].reshape(BUF, half)
         into[:, side * half : (side + 1) * half] = part.astype(BF)
@@ -231,6 +238,28 @@
         axis, known = self.order[phase], self.order[:phase]
         got = self.region(known, self.place.moved(axis, 4 - k))
         self.forwards.append(self.copies.go(got, got, self.place.twin))
+
+    def start_relay(self, phase):
+        axis, known = self.order[phase], self.order[:phase]
+        here = self.region(known, self.place.at)
+        self.phases.append([self.copies.go(here, here, self.place.peer(axis, k)) for k in (1, 3)])
+
+    def arrive_relay(self, phase):
+        axis, known = self.order[phase], self.order[:phase]
+        lanes, middle = self.lanes, (self.lanes.size // 256) * 128
+        relayed = []
+        for copy, k, start, size in zip(
+            self.phases[phase], (1, 3), (lanes.start, lanes.start + middle), (middle, lanes.size - middle)
+        ):
+            copy.wait_recv()
+            self.lanes = pl.ds(start, size)
+            got = self.region(known, self.place.moved(axis, 4 - k))
+            relayed.append(self.copies.go(got, got, self.place.peer(axis, k)))
+            self.lanes = lanes
+            self.forward(phase, k)
+        for copy in relayed:
+            copy.wait_recv()
+        self.forward(phase, 2)
 
     def arrive(self, phase, forward=False):
         for k, copy in enumerate(self.phases[phase]):
@@ -335,44 +364,59 @@
 
 
 def gather_kernel(
-    x_ref, wq_ref, wk_ref, wv_ref, wo_ref, small_ref,
-    normed_ref, land_ref, wq_out, wk_out, wv_out, wo_out, wr_out, gain_out, tab_out,
-    box, out_ref, send_sem, recv_sem, trade_send, trade_recv,
+    x_ref, wq_ref, wk_ref, wv_ref, wo_ref, small_ref, place_ref, dy_ref,
+    normed_ref, land_ref, dy_land, dy_rest, wq_out, wk_out, wv_out, wo_out, wr_out, gain_out, tab_out,
+    box, out_ref, dy_hold, send_sem, recv_sem, *sems,
 ):
     place = Place()
     z, y, x, c = place.z, place.y, place.x, place.c
-    for k, w_ref in enumerate((wq_ref, wk_ref, wv_ref, wo_ref)):
-        box[z, y, x, c, :, k * HALF : (k + 1) * HALF] = folded(w_ref[...].astype(F32)).astype(BF)
-    box[z, y, x, c, :, 4 * HALF :] = small_ref[...]
+    for at, w_ref in ((0, wq_ref), (HALF, wk_ref), (2 * HALF, wv_ref), (OUT, wo_ref)):
+        box[z, y, x, c, :, at : at + HALF] = folded(w_ref[...].astype(F32)).astype(BF)
+    box[z, y, x, c, :, SMALL:OUT] = small_ref[...]
     greet(plane_peers() + place.peers("x") + [place.twin])
     copies = Copies(send_sem, recv_sem)
-    trade = Exchange(out_ref, land_ref, trade_send, trade_recv)
+    trade = Exchange(out_ref, land_ref, sems[0], sems[1])
+    early = Exchange(dy_hold, dy_land, sems[2], sems[3])
     both = [Gather(place, box, copies, lanes, order) for lanes, order in GATHER_PARTS]
+    late = [Gather(place, box, copies, lanes, order) for lanes, order in LATE_PARTS]
     for part in both:
         part.start(0)
-    for part in both:
+    for part in both + late:
         part.forward_own()
+    for part in late:
+        part.start(0)
     tokens = x_ref[...].astype(F32)
     unit = tokens * lax.rsqrt(jnp.mean(tokens * tokens, axis=-1, keepdims=True) + EPS)
-    for phase in (0, 1):
-        for part in both:
-            part.arrive(phase)
-            part.start(phase + 1)
-        for part in both:
-            part.forward_all(phase)
     for part in both:
-        part.arrive(2, forward=True)
+        part.arrive(0)
+        part.start(1)
+    for part in both:
+        part.forward_all(0)
+    for part in both:
+        part.arrive(1)
+        part.start_relay(2)
+    for part in both:
+        part.forward_all(1)
+    dy_rows = spread(nn(place_ref[...], dy_ref[...]))
+    dy_hold[...] = dy_rows[:, :EARLY]
+    dy_rest[...] = dy_rows[:, EARLY:]
+    for part in both:
+        part.arrive_relay(2)
+    for part in late:
+        part.arrive(0, forward=True)
+        part.start(1)
+    early.start()
     for part in both:
         part.finish()
 
-    def unfold(k, w_out):
+    def unfold(at, w_out):
         for plane in range(4):
-            value = box[plane, :, :, :, :, k * HALF : (k + 1) * HALF].reshape(32, 16, HALF)
+            value = box[plane, :, :, :, :, at : at + HALF].reshape(32, 16, HALF)
             unfold_into(w_out, plane, value.astype(F32))
 
     for k, w_out in enumerate((wq_out, wk_out, wv_out)):
-        unfold(k, w_out)
-    small = box[:, :, :, :, :, 4 * HALF :].reshape(128, 16, 128).astype(F32)
+        unfold(k * HALF, w_out)
+    small = box[:, :, :, :, :, SMALL:OUT].reshape(128, 16, 128).astype(F32)
     lane = lax.broadcasted_iota(jnp.int32, (D, 128), 1)
     wr_out[...] = jnp.where(lane < EXPERTS, small[:, :8, :].reshape(D, 128), 0.0).astype(BF)
     pick, mine = lane_pick(), own_columns()
@@ -381,7 +425,7 @@
         for row in range(2)
     ]
     gain_out[...] = jnp.concatenate(gains + [jnp.zeros((6, D), F32)], axis=0)
-    near = box[z, y, :, :, :, 4 * HALF :].reshape(8, 16, 128).astype(F32)
+    near = box[z, y, :, :, :, SMALL:OUT].reshape(8, 16, 128).astype(F32)
     tab_out[...] = pick_row(near, 10)
 
     normed = (unit * gains[0]).astype(BF)
@@ -396,14 +440,24 @@
                 first, second = pack_pair(res[:TS, cols], res[TS:, cols])
                 out_ref[head, which * TS : (which + 1) * TS, :] = first
                 out_ref[head + 1, which * TS : (which + 1) * TS, :] = second
+        if k == 1:
+            for part_late in late:
+                part_late.arrive(1, forward=True)
+                part_late.start(2)
         for j in (1, 2, 3, 0):
             if k or j:
                 trade.copy(part * 4 + ring(y, j)).start()
             else:
                 trade.keep()
-    unfold(3, wo_out)
+    for part in late:
+        part.arrive(2, forward=True)
+    for part in late:
+        part.finish()
+    unfold(OUT, wo_out)
     trade.arrive()
+    early.arrive()
     trade.drain()
+    early.drain()
     copies.drain()
 
 
@@ -452,12 +506,19 @@
     ).astype(BF)
 
 
-def loop(strip, low, high, count):
-    def body(i, carry):
-        strip(i, count, i - 8 if count == 9 else 0)
-        return carry
-
-    lax.fori_loop(low, high, body, 0)
+def strips(strip, after):
+    def run(low, count):
+        def body(at, carry):
+            i = low + at
+            strip(i + 8, 9, i)
+            strip(i, count, 0)
+            after(i)
+            return carry
+
+        lax.fori_loop(0, 4, body, 0)
+
+    run(0, 4)
+    run(4, 8)
 
 
 def span(block, count):
@@ -465,10 +526,12 @@
 
 
 def attn_fwd_kernel(
-    len_ref, tab_ref, recv_ref, land_ref, lse_ref, kext, qext, bias, vt, out_ref, send_sem, recv_sem
+    len_ref, tab_ref, recv_ref, dy_ref, land_ref, lse_ref, dy_land, kext, qext, bias, vt, out_ref, *sems
 ):
     greet(plane_peers())
-    trade = Exchange(out_ref, land_ref, send_sem, recv_sem)
+    trade = Exchange(out_ref, land_ref, sems[0], sems[1])
+    early = Exchange(dy_ref, dy_land, sems[2], sems[3])
+    early.start()
     attn_setup(len_ref, tab_ref, recv_ref, kext, qext, bias)
     unit = eye(TS)
     for i in range(EXPERTS):
@@ -483,13 +546,16 @@
         both = jnp.concatenate([res[:HD, :TS], res[HD:, TS:]], axis=0)
         out_ref[i] = both.T.astype(BF)
         lse_ref[i] = jnp.broadcast_to(top + jnp.log(total), (8, TOK))
+
+    def after(i):
+        trade.push(i + 8)
         trade.push(i)
 
-    loop(strip, 0, 4, 4)
-    loop(strip, 4, 8, 8)
-    loop(strip, 8, 16, 9)
+    strips(strip, after)
     trade.arrive()
+    early.arrive()
     trade.drain()
+    early.drain()
 
 
 def attn_bwd_kernel(
@@ -528,53 +594,52 @@
         dqt = nn(ktext[:, span(first, count)], ds)
         both = jnp.concatenate([dqt[:HD, :TS], dqt[HD : 2 * HD, TS:]], axis=0) * (HD**-0.5)
         out_ref[i, 0:TS, :] = both.T.astype(BF)
-        trade_q.push(i)
         far[...] += dqt[128:136]
         if count == 9:
             near[...] += ds[7 * TS :].astype(F32)
         else:
-            nearby.append(ds)
-
-    nearby = []
-
-    def finish(block):
-        out_ref[block, TS : 2 * TS, :] = dk[span(block, 1), :].astype(BF)
-        out_ref[block, 2 * TS :, :] = dv[span(block, 1), :].astype(BF)
-        trade_kv.push(block)
-
-    def sweep(low, high, count):
-        def body(i, carry):
-            nearby.clear()
-            first = i - 8 if count == 9 else 0
-            strip(i, count, first)
-            if count == 9:
-                finish(first)
-            else:
-                ds = nearby[0]
-                for block in range(count):
-                    value = ds[block * TS : (block + 1) * TS].astype(F32)
-
-                    @pl.when(i == block)
-                    def _(value=value):
-                        near[TS:] += value
-
-                    @pl.when(i == block + 1)
-                    def _(value=value):
-                        near[:TS] += value
-
+            for block in range(count):
+                value = ds[block * TS : (block + 1) * TS].astype(F32)
+                near[TS:] += value * (i == block).astype(F32)
+                near[:TS] += value * (i == block + 1).astype(F32)
+
+    def finish(i):
+        out_ref[i, TS : 2 * TS, :] = dk[span(i, 1), :].astype(BF)
+        out_ref[i, 2 * TS :, :] = dv[span(i, 1), :].astype(BF)
+        trade_kv.push(i)
+
+    odd = lax.rem(trade_kv.me, 2)
+
+    def first_half(low, count):
+        def body(at, carry):
+            i = low + 2 * at
+            strip(i, count, 0)
+            strip(i + 1, count, 0)
+            trade_q.push(i)
+            trade_q.push(i + 1)
             return carry
 
-        lax.fori_loop(low, high, body, 0)
-
-    sweep(0, 4, 4)
-    sweep(4, 8, 8)
-    sweep(8, 16, 9)
-
-    def rest(block, carry):
-        finish(block)
+        lax.fori_loop(0, 2, body, 0)
+
+    first_half(0, 4)
+    first_half(4, 8)
+
+    def second_half(at, carry):
+        blocks = [odd * (8 + step) + (1 - odd) * (15 - step) for step in (2 * at, 2 * at + 1)]
+        for i in blocks:
+            strip(i, 9, i - 8)
+        for i in blocks:
+            trade_q.push(i)
+            finish(i - 8 * odd)
         return carry
 
-    lax.fori_loop(8, EXPERTS, rest, 0)
+    lax.fori_loop(0, 4, second_half, 0)
+
+    def rest(step, carry):
+        finish(lax.rem(step + lax.div(trade_kv.me, 2), 8) + 8 * odd)
+        return carry
+
+    lax.fori_loop(0, 8, rest, 0)
     grads = near[:, :TS] + near[:, TS:]
     dist = (
         TS
@@ -617,25 +682,44 @@
     return jnp.sum(jnp.where(own, nn(place, high) + nn(place, low), 0.0), axis=1, keepdims=True)
 
 
-FFC = 2 * SHARD
-STEPS = FF // FFC
+CHUNKS = ((0, 768), (768, 768), (1536, 768), (2304, 512))
+
+
+def pieces(at, size):
+    found, row = [], at
+    while row < at + size:
+        end = min(at + size, (row // SHARD + 1) * SHARD)
+        found.append((row // SHARD, row % SHARD, row - at, end - row))
+        row = end
+    return found
+
+
+STAGED = 3 * sum(len(pieces(at, size)) for at, size in CHUNKS)
 
 
 def moe_kernel(
-    recv_ref, x_ref, wo_ref, gain_ref, wr_ref, mask_ref, place_ref, dy_ref, w_ref,
+    recv_ref, x_ref, wo_ref, gain_ref, wr_ref, mask_ref, place_ref, dy_ref, dy_late_ref, w_ref,
     att_ref, hidden_ref, mixed_ref, share_ref, back_out, back_row, grads_ref,
-    w_buf, hold_a, hold_b, land_a, land_b, rows, slots, act, first, second, acc, stage,
+    w_buf, hold_a, hold_b, land_a, hold_s, land_s, rows, slots, act, first, second, acc, stage,
     w_sem, stage_sem, *sems,
 ):
-    def load(step):
-        slot = lax.rem(step, 2)
-        return pltpu.make_async_copy(w_ref.at[pl.ds(step * 2, 2)], w_buf.at[slot], w_sem.at[slot])
-
-    load(0).start()
-    load(1).start()
+    loads = [
+        [
+            pltpu.make_async_copy(
+                w_ref.at[s, pl.ds(k * SHARD, SHARD)],
+                w_buf.at[k, pl.ds(s * SHARD, SHARD)],
+                w_sem.at[k * FSDP + s],
+            )
+            for s in range(FSDP)
+        ]
+        for k in range(3)
+    ]
+    for k in (2, 0, 1):
+        for copy in loads[k]:
+            copy.start()
     greet(plane_peers())
     to_rows = Exchange(hold_a, land_a, sems[0], sems[1])
-    to_slots = Exchange(hold_b, land_b, sems[2], sems[3])
+    to_shares = Exchange(hold_s, land_s, sems[2], sems[3])
     from_out = Exchange(hold_a, back_out, sems[4], sems[5])
     from_row = Exchange(hold_b, back_row, sems[6], sems[7])
 
@@ -657,22 +741,27 @@
     weight = jnp.exp(logits - jnp.max(logits, axis=1, keepdims=True))
     share = weight / jnp.sum(weight, axis=1, keepdims=True)
     share_ref[...] = share
-    hold_b[...] = spread(slot_share(place, share, row_expert()) * nn(place, dy_ref[...]))
-
+    high, low = halves(slot_share(place, share, row_expert()))
+    lane = lax.broadcasted_iota(jnp.int32, (BUF, 128), 1)
+    value = jnp.where(lane == 0, high.astype(F32), 0.0) + jnp.where(lane == 1, low.astype(F32), 0.0)
+    value = value.reshape(EXPERTS, 2 * CAP, 128)
+    hold_s[...] = jnp.concatenate([value, jnp.zeros((EXPERTS, 8, 128), F32)], axis=1).astype(BF)
+    to_shares.start()
+
+    unspread(slots, dy_ref, dy_late_ref)
+    for copy in loads[2]:
+        copy.wait()
+    for at, size in CHUNKS:
+        first[:, at : at + size] = nt(slots[...], w_buf[2, at : at + size, :]).astype(BF)
+    for k in range(2):
+        for copy in loads[k]:
+            copy.wait()
     to_rows.arrive()
-    to_slots.start()
-    unspread(land_a, rows)
-    acc[...] = jnp.zeros_like(acc)
-
-    def weights(step):
-        w = w_buf[lax.rem(step, 2)]
-        return [w[:, k * SHARD : (k + 1) * SHARD, :].reshape(FFC, D) for k in range(3)]
-
-    def forward(step, carry):
-        load(step).wait()
-        gate_w, up_w, down_w = weights(step)
-        gate = nt(rows[...], gate_w)
-        up = nt(rows[...], up_w)
+    unspread(rows, land_a)
+    for at, size in CHUNKS:
+        cols = slice(at, at + size)
+        gate = nt(rows[...], w_buf[0, cols, :])
+        up = nt(rows[...], w_buf[1, cols, :])
         square = gate * gate
         tanh = jnp.tanh(GELU_C * gate * (1.0 + 0.044715 * square))
         half_up = 0.5 * (1.0 + tanh)
@@ -680,78 +769,54 @@
         slope = half_up + 0.5 * gate * (1.0 - tanh * tanh) * (
             GELU_C * (1.0 + 3 * 0.044715 * square)
         )
-        acted = (gelu * up).astype(BF)
-        act[step] = acted
-        first[step] = (up * slope).astype(BF)
-        second[step] = gelu.astype(BF)
-        acc[...] += nn(acted, down_w)
-
-        @pl.when(step < STEPS - 2)
-        def _():
-            load(step + 2).start()
-
-        return carry
-
-    lax.fori_loop(0, STEPS, forward, 0)
+        act_grad = first[:, cols].astype(F32)
+        act[:, cols] = (gelu * up).astype(BF)
+        first[:, cols] = (act_grad * up * slope).astype(BF)
+        second[:, cols] = (act_grad * gelu).astype(BF)
+    for half in range(2):
+        cols = slice(half * HALF, half * HALF + HALF)
+        acc[:, cols] = nn(act[...], w_buf[2, :, cols])
     to_rows.drain()
     hold_a[...] = spread(acc[...])
     from_out.start()
-    to_slots.arrive()
-    unspread(land_b, slots)
-    acc[...] = jnp.zeros_like(acc)
-
-    def backward(at, carry):
-        step = STEPS - 1 - at
-
-        @pl.when(at >= 2)
-        def _():
-            load(step).wait()
-
-        gate_w, up_w, down_w = weights(step)
-        act_grad = nt(slots[...], down_w).astype(BF).astype(F32)
-        gate_grad = (act_grad * first[step].astype(F32)).astype(BF)
-        up_grad = (act_grad * second[step].astype(F32)).astype(BF)
-        first[step] = gate_grad
-        second[step] = up_grad
-        acc[...] += nn(gate_grad, gate_w) + nn(up_grad, up_w)
-
-        @pl.when(at < 2)
-        def _():
-            load(step - 2).start()
-
-        return carry
-
-    lax.fori_loop(0, STEPS, backward, 0)
-    to_slots.drain()
+    for half in range(2):
+        cols = slice(half * HALF, half * HALF + HALF)
+        acc[:, cols] = nn(first[...], w_buf[0, :, cols]) + nn(second[...], w_buf[1, :, cols])
     hold_b[...] = spread(acc[...])
     from_row.start()
 
-    def store(step, which):
-        return pltpu.make_async_copy(
-            stage.at[which],
-            grads_ref.at[pl.ds(step * 2, 2), pl.ds(which * SHARD, SHARD)],
-            stage_sem.at[which],
-        )
-
-    def weight_grads(step, carry):
-        for which, (left, right) in enumerate(((first, rows), (second, rows), (act, slots))):
-            value = tn(left[step], right[...]).astype(BF).reshape(2, SHARD, D)
-
-            @pl.when(step > 0)
-            def _(which=which):
-                store(step - 1, which).wait()
-
-            stage[which] = value
-            store(step, which).start()
-        return carry
-
-    lax.fori_loop(0, STEPS, weight_grads, 0)
-    for which in range(3):
-        store(STEPS - 1, which).wait()
+    to_shares.arrive()
+    value = land_s[...].astype(F32)[:, : 2 * CAP, :].reshape(BUF, 128)
+    scale = jnp.sum(value, axis=1, keepdims=True)
+    rows[...] = (rows[...].astype(F32) * scale).astype(BF)
+    slots[...] = (slots[...].astype(F32) * scale).astype(BF)
+    pending = [[], [], []]
+    count = turn = 0
+    for which, (left, right) in ((2, (act, slots)), (0, (first, rows)), (1, (second, rows))):
+        for at, size in CHUNKS:
+            value = tn(left[:, at : at + size], right[...]).astype(BF)
+            for copy in pending[turn]:
+                copy.wait()
+            stage[turn, :size, :] = value
+            pending[turn] = []
+            for shard, row, local, amount in pieces(at, size):
+                copy = pltpu.make_async_copy(
+                    stage.at[turn, pl.ds(local, amount)],
+                    grads_ref.at[shard, pl.ds(which * SHARD + row, amount)],
+                    stage_sem.at[count],
+                )
+                copy.start()
+                pending[turn].append(copy)
+                count += 1
+            turn = (turn + 1) % 3
+    for group in pending:
+        for copy in group:
+            copy.wait()
     from_out.arrive()
     from_row.arrive()
     from_out.drain()
     from_row.drain()
+    to_shares.drain()
 
 
 def back_kernel(
@@ -762,8 +827,8 @@
     greet(plane_peers())
     z, y, _, _ = coords()
     trade = Exchange(send_ref, land_ref, send_sem, recv_sem)
-    unspread(out_ref, outs)
-    unspread(row_ref, rows)
+    unspread(outs, out_ref)
+    unspread(rows, row_ref)
     place = place_ref[...]
     place_t = place_t_ref[...]
     own = row_expert()
@@ -776,7 +841,12 @@
     inner = jnp.sum(share * share_grad, axis=1, keepdims=True)
     lg_high, lg_low = halves(share * (share_grad - inner))
     wr = wr_ref[...]
-    mixed_grad = nn(place_t, rows[...]) + (nt(lg_high, wr) + nt(lg_low, wr))
+    scale_high, scale_low = halves(
+        place_t.astype(F32) * slot_share(place, share, own).T
+    )
+    mixed_grad = (nn(scale_high, rows[...]) + nn(scale_low, rows[...])) + (
+        nt(lg_high, wr) + nt(lg_low, wr)
+    )
     hidden = hidden_ref[...]
     factor = lax.rsqrt(jnp.mean(hidden * hidden, axis=-1, keepdims=True) + EPS)
     unit = hidden * factor
@@ -804,9 +874,6 @@
                 trade.keep()
     mixed = mixed_ref[...]
     router_ref[...] = tn(mixed, lg_high) + tn(mixed, lg_low)
-    scale_high, scale_low = halves(
-        place_t.astype(F32) * slot_share(place, share, own).T
-    )
     moe = nn(scale_high, returned) + nn(scale_low, returned)
     result_ref[...] = (hidden + moe).astype(BF)
     trade.arrive()
@@ -821,13 +888,13 @@
     place = Place()
     z, y, c = place.z, place.y, place.c
     greet(place.peers("xyz") + [place.twin])
-    copies = Copies(rest[15], rest[16])
+    copies = Copies(rest[20], rest[21])
     parts = [
         Reduce(
             place, copies, order, (from_twin, lanes),
             [(bufs[0], pl.ds(0, lanes.size)), (bufs[1], pl.ds(0, lanes.size))], bufs[2:],
         )
-        for (lanes, order), bufs in zip(REDUCE_PARTS, (rest[0:5], rest[5:10], rest[10:15]))
+        for (lanes, order), bufs in zip(REDUCE_PARTS, (rest[0:5], rest[5:10], rest[10:15], rest[15:20]))
     ]
     flats = (flat_q, flat_k, flat_v)
     for which, flat in enumerate(flats):
@@ -838,40 +905,56 @@
 
         unpack_heads(recv_ref, which * TS, emit)
 
-    total = nt(flat_q[...], wq_ref[...]) + nt(flat_k[...], wk_ref[...]) + nt(flat_v[...], wv_ref[...])
-    tokens = x_ref[...].astype(F32)
-    factor = lax.rsqrt(jnp.mean(tokens * tokens, axis=-1, keepdims=True) + EPS)
-    unit = tokens * factor
-
-    at = lax.broadcasted_iota(jnp.int32, (128, 8, 128), 1)
-    gains = [by_device(row) for row in (jnp.sum(total * unit, axis=0, keepdims=True), moe_gain_ref[0:1, :])]
-    lower = jnp.where(at == 0, gains[0][:, None, :], 0.0) + jnp.where(at == 1, gains[1][:, None, :], 0.0)
-    extra = jnp.concatenate([router_ref[...].reshape(128, 8, 128), lower], axis=1)
-    box[:, :, :, :, :, 4 * HALF :] = extra.astype(BF).reshape(4, 4, 4, 2, 16, 128)
-    at = lax.broadcasted_iota(jnp.int32, (8, 16, 128), 1)
-    here = box[z, y, :, :, :, 4 * HALF :].reshape(8, 16, 128).astype(F32)
-    here = here + jnp.where(at == 10, table_ref[...][:, None, :], 0.0)
-    box[z, y, :, :, :, 4 * HALF :] = here.astype(BF).reshape(4, 2, 16, 128)
-
     planes = [ring(z, k) for k in (1, 2, 3, 0)]
     to_twin = []
-    for plane in planes:
+
+    def pair_sum(k):
+        plane = planes[k]
+        to_twin[k].wait_recv()
+        both = box[plane, :, :, c, :, MAIN].astype(F32) + from_twin[plane, :, :, :, MAIN].astype(F32)
+        from_twin[plane, :, :, :, MAIN] = both.astype(BF)
+        if k < 3:
+            parts[0].send(0, k + 1)
+
+    for k, plane in enumerate(planes):
         cols = pl.ds(pl.multiple_of(plane * 256, 256), 256)
         for which, (left, flat) in enumerate(
             ((normed_ref, flat_q), (normed_ref, flat_k), (normed_ref, flat_v), (att_ref, branch_ref))
         ):
             value = fold_rows(tn(left[:, cols], flat[...])).astype(BF)
             box[plane, :, :, :, :, which * HALF : (which + 1) * HALF] = value.reshape(4, 4, 2, 16, HALF)
-        to_twin.append(copies.go(box.at[plane, :, :, 1 - c], from_twin.at[plane], place.twin))
-
-    for k, plane in enumerate(planes):
-        to_twin[k].wait_recv()
-        both = box[plane, :, :, c].astype(F32) + from_twin[plane].astype(F32)
-        from_twin[plane] = both.astype(BF)
-        if k < 3:
-            parts[0].send(0, k + 1)
+        to_twin.append(
+            copies.go(
+                box.at[plane, :, :, 1 - c, :, MAIN], from_twin.at[plane, :, :, :, MAIN], place.twin
+            )
+        )
+        if k:
+            pair_sum(k - 1)
+    pair_sum(3)
     parts[1].start(0)
     parts[2].start(0)
+
+    total = nt(flat_q[...], wq_ref[...]) + nt(flat_k[...], wk_ref[...]) + nt(flat_v[...], wv_ref[...])
+    tokens = x_ref[...].astype(F32)
+    factor = lax.rsqrt(jnp.mean(tokens * tokens, axis=-1, keepdims=True) + EPS)
+    unit = tokens * factor
+
+    at = lax.broadcasted_iota(jnp.int32, (128, 8, 128), 1)
+    gains = [by_device(row) for row in (jnp.sum(total * unit, axis=0, keepdims=True), moe_gain_ref[0:1, :])]
+    lower = jnp.where(at == 0, gains[0][:, None, :], 0.0) + jnp.where(at == 1, gains[1][:, None, :], 0.0)
+    extra = jnp.concatenate([router_ref[...].reshape(128, 8, 128), lower], axis=1)
+    box[:, :, :, :, :, REST] = extra.astype(BF).reshape(4, 4, 4, 2, 16, 128)
+    at = lax.broadcasted_iota(jnp.int32, (8, 16, 128), 1)
+    here = box[z, y, :, :, :, REST].reshape(8, 16, 128).astype(F32)
+    here = here + jnp.where(at == 10, table_ref[...][:, None, :], 0.0)
+    box[z, y, :, :, :, REST] = here.astype(BF).reshape(4, 2, 16, 128)
+    rest_copy = copies.go(
+        box.at[:, :, :, 1 - c, :, REST], from_twin.at[:, :, :, :, REST], place.twin
+    )
+    rest_copy.wait_recv()
+    both = box[:, :, :, c, :, REST].astype(F32) + from_twin[:, :, :, :, REST].astype(F32)
+    from_twin[:, :, :, :, REST] = both.astype(BF)
+    parts[3].start(0)
     scaled = total * gains_ref[0:1, :]
     igrad_ref[...] = (
         hgrad_ref[...]
@@ -888,6 +971,17 @@
     copies.drain()
 
 
+def emit_kernel(expert_ref, sum_ref, gate, up, down, gq, gk, gv, go, router, gain_attn, gain_moe, table):
+    for k, ref in enumerate((gate, up, down)):
+        ref[...] = expert_ref[k * SHARD : (k + 1) * SHARD, :].astype(F32)
+    for k, ref in enumerate((gq, gk, gv, go)):
+        ref[...] = sum_ref[k * 8 : k * 8 + 8, :]
+    router[...] = sum_ref[32:40, :EXPERTS]
+    gain_attn[...] = sum_ref[40:41, :8]
+    gain_moe[...] = sum_ref[41:42, :8]
+    table[...] = sum_ref[42:43, :4]
+
+
 def placement(routes, order):
     micro = routes.shape[0]
     slots = routes.reshape(micro, 2 * TS)
@@ -928,21 +1022,23 @@
     dy = cotangent.reshape(TOK, D)
     lengths = doc_lengths[:, 0]
 
-    normed, heads, wq, wk, wv, wo, wr, gains, table = call(
+    chunk = (EXPERTS, 4 * CAP, HALF)
+    early, rest = (EXPERTS, EARLY, HALF), (EXPERTS, 4 * CAP - EARLY, HALF)
+    normed, heads, dy_early, dy_rest, wq, wk, wv, wo, wr, gains, table = call(
         gather_kernel,
         (
-            shape((TOK, D), BF), shape((H, 3 * TS, 128), BF), shape((D, D), BF), shape((D, D), BF),
+            shape((TOK, D), BF), shape((H, 3 * TS, 128), BF), shape(early, BF), shape(rest, BF), shape((D, D), BF), shape((D, D), BF),
             shape((D, D), BF), shape((D, D), BF), shape((D, 128), BF), shape((8, D), F32), shape((8, 128), F32),
         ),
-        x, w_query, w_key, w_value, w_out, small,
+        x, w_query, w_key, w_value, w_out, small, place, dy,
         scratch=[
             pltpu.VMEM((4, 4, 4, 2, 16, WIDE), BF),
             pltpu.VMEM((H, 3 * TS, 128), BF),
-            pltpu.SemaphoreType.DMA((57,)),
-            pltpu.SemaphoreType.DMA((57,)),
-            pltpu.SemaphoreType.DMA((EXPERTS,)),
-            pltpu.SemaphoreType.DMA((EXPERTS,)),
-        ],
+            pltpu.VMEM(early, BF),
+            pltpu.SemaphoreType.DMA((78,)),
+            pltpu.SemaphoreType.DMA((78,)),
+        ]
+        + [pltpu.SemaphoreType.DMA((EXPERTS,))] * 4,
         collective_id=1,
     )
     smem = pl.BlockSpec(memory_space=pltpu.SMEM)
@@ -952,17 +1048,16 @@
         pltpu.VMEM((EXPERTS, TOK, 256), BF),
         pltpu.VMEM((12 * TS, TOK), F32),
     ]
-    att_back, lse = call(
+    att_back, lse, dy_late = call(
         attn_fwd_kernel,
-        (shape((EXPERTS, TS, 128), BF), shape((EXPERTS, 8, TOK), F32)),
-        lengths, table, heads,
-        in_specs=[smem, vmem, vmem],
+        (shape((EXPERTS, TS, 128), BF), shape((EXPERTS, 8, TOK), F32), shape(rest, BF)),
+        lengths, table, heads, dy_rest,
+        in_specs=[smem] + [vmem] * 3,
         scratch=attn_scratch
         + [pltpu.VMEM((128, SEQ), BF), pltpu.VMEM((EXPERTS, TS, 128), BF)]
-        + [pltpu.SemaphoreType.DMA((EXPERTS,))] * 2,
+        + [pltpu.SemaphoreType.DMA((EXPERTS,))] * 4,
         collective_id=5,
     )
-    chunk = (EXPERTS, 4 * CAP, D // 2)
     anywhere = pl.BlockSpec(memory_space=pl.ANY)
     att, hidden, mixed, share, outs, row_grads, expert_grads = call(
         moe_kernel,
@@ -970,17 +1065,18 @@
             shape((TOK, D), BF), shape((TOK, D), F32), shape((TOK, D), BF), shape((TOK, 128), F32),
             shape(chunk, BF), shape(chunk, BF), shape((FSDP, 3 * SHARD, D), BF),
         ),
-        att_back, x, wo, gains, wr, picked, place, dy, expert_w,
-        in_specs=[vmem] * 8 + [anywhere],
+        att_back, x, wo, gains, wr, picked, place, dy_early, dy_late, expert_w,
+        in_specs=[vmem] * 9 + [anywhere],
         out_specs=(vmem,) * 6 + (anywhere,),
         scratch=[
-            pltpu.VMEM((2, 2, 3 * SHARD, D), BF),
-            pltpu.VMEM(chunk, BF), pltpu.VMEM(chunk, BF), pltpu.VMEM(chunk, BF), pltpu.VMEM(chunk, BF),
+            pltpu.VMEM((3, FF, D), BF),
+            pltpu.VMEM(chunk, BF), pltpu.VMEM(chunk, BF), pltpu.VMEM(chunk, BF),
+            pltpu.VMEM((EXPERTS, 48, 128), BF), pltpu.VMEM((EXPERTS, 48, 128), BF),
             pltpu.VMEM((BUF, D), BF), pltpu.VMEM((BUF, D), BF),
-            pltpu.VMEM((STEPS, BUF, FFC), BF), pltpu.VMEM((STEPS, BUF, FFC), BF), pltpu.VMEM((STEPS, BUF, FFC), BF),
+            pltpu.VMEM((BUF, FF), BF), pltpu.VMEM((BUF, FF), BF), pltpu.VMEM((BUF, FF), BF),
             pltpu.VMEM((BUF, D), F32),
-            pltpu.VMEM((3, 2, SHARD, D), BF),
-            pltpu.SemaphoreType.DMA((2,)), pltpu.SemaphoreType.DMA((3,)),
+            pltpu.VMEM((3, 768, D), BF),
+            pltpu.SemaphoreType.DMA((3 * FSDP,)), pltpu.SemaphoreType.DMA((STAGED,)),
         ]
         + [pltpu.SemaphoreType.DMA((EXPERTS,))] * 8,
         collective_id=3,
@@ -1028,23 +1124,20 @@
             pltpu.VMEM((4, 4, 4, 16, WIDE), BF),
         ]
         + [buf for lanes, _ in REDUCE_PARTS for buf in reduce_scratch(lanes.size)]
-        + [pltpu.SemaphoreType.DMA((31,))] * 2,
+        + [pltpu.SemaphoreType.DMA((41,))] * 2,
         collective_id=2,
     )
+    block = shape((SHARD, D), F32)
+    rows = shape((8, D), F32)
+    gate, up, down, gq, gk, gv, go, router, gain_a, gain_m, table_sum = call(
+        emit_kernel,
+        (block, block, block, rows, rows, rows, rows)
+        + tuple(shape(dims, F32) for dims in ((8, EXPERTS), (1, 8), (1, 8), (1, 4))),
+        expert_sum, sums,
+    )
     return (
-        result.reshape(tokens.shape),
-        input_grad.reshape(tokens.shape),
-        sums[40, :8],
-        sums[0:8],
-        sums[8:16],
-        sums[16:24],
-        sums[24:32],
-        sums[42, :4],
-        sums[41, :8],
-        sums[32:40, :EXPERTS],
-        expert_sum[:SHARD].astype(F32).T[None],
-        expert_sum[SHARD : 2 * SHARD].astype(F32).T[None],
-        expert_sum[2 * SHARD :].astype(F32)[None],
+        result.reshape(tokens.shape), input_grad.reshape(tokens.shape), gain_a[0], gq, gk, gv, go,
+        table_sum[0], gain_m[0], router, gate.T[None], up.T[None], down[None],
     )
 
 

time: 347 us -> 336 us (0.968)
  local copies, waits for them, and re-layouts: 9.17 us -> 4.25 us
  other arithmetic: 9.77 us -> 6.11 us
    broadcast_in_dim x1 -> x0, other arithmetic: 3.84 us -> none  [on_device(): expert_sum[2 * SHARD:].astype(F32)[None]]
    pallas_call x6 -> x7, Pallas kernels: 309 us -> 308 us  [call(): pl.pallas_call(kernel, out_shape=out_shape, in_specs=in_specs or [pl.Bloc...]
  transfers between devices with their start and end apart: 2 -> 2, of which waited for: 0 -> 0; matrix products, arithmetic and copies ran while one was open for 3% -> 2% of each run, Pallas kernels for 64% -> 68%
where the time goes in v1:
time: 336 us; the launch traced here: 333 us
  Pallas kernels  308 us (92%)
  between operations  14.5 us (4%)
  other arithmetic  6.11 us (2%)
  local copies, waits for them, and re-layouts  4.25 us (1%)
    pallas_call x7, Pallas kernels, call(): pl.pallas_call(kernel, out_shape=out_shape, in_specs=in_specs or [pl.Bloc...  308 us
  transfers between devices with their start and end apart: 2, of which 0 were waited for; matrix products, arithmetic and copies ran while one was open for 2% of the time, Pallas kernels for 68%

profile of v1, /device:TPU:1, one launch (start us, length us, event | category | flops | bytes accessed | tf_op | source)
XLA Modules:
  0.0 332.7 jit_solution(1686178577986599976)
XLA Ops:
  7.2 3.1 pad_maximum_fusion
  10.4 0.0 reduce-scatter.2.cloned.1.call-start
  10.5 0.6 copy-done.2
  11.1 0.1 copy.35
  11.2 0.1 copy.36
  11.3 0.1 eq.102
  11.5 0.3 convert_reduce_fusion
  11.8 0.1 reduce_sum.12
  12.1 1.2 concatenate.6.small_ref
  13.3 0.1 broadcast_bitcast_fusion
  13.3 0.1 add_select_fusion
  13.5 0.2 slice_reduce_fusion.1
  13.7 0.9 fusion.1.place_ref
  14.5 84.0 %shard_map.255 = (bf16[256,1024]{1,0:T(8,128)(2,1)}, bf16[16,384,128]{2,1,0:T(8,128)(2,1)}, bf16[16,32,512]{2,1,0:T(8,128)(2,1)}, bf16[16,48,512]{2,1,0:T(8,128)...) custom-call(bf16[256,1024]{1,0:T(8,128)(2,1)} %bitcast.45, ...), custom_call_target="tpu_custom_call" | custom-call | tf_op jit(solution)/shard_map/pallas_call | solution.py:49
  98.6 25.6 %shard_map.256 = (bf16[16,128,128]{2,1,0:T(8,128)(2,1)}, f32[16,8,256]{2,1,0:T(8,128)}, bf16[16,48,512]{2,1,0:T(8,128)(2,1)}) custom-call(s32[2,3]{1,0:T(2,128)} %bitcast.58, f32[8,128]{1,0:T(8,128)} %get-tuple-element.55.tab_ref, bf16[16,384,128]{2,1,0:T(8,128)(2,1)} %get-tuple-element.56.recv_ref, bf16[16,48,512]{2,1,0:T(8,128)(2,1)} %get-tuple-element.57.dy_ref), custom_call_target="tpu_custom_call" | custom-call | tf_op jit(solution)/shard_map/pallas_call | solution.py:49
  124.2 0.8 fusion.5.mask_ref
  125.0 77.8 %shard_map.257 = (bf16[256,1024]{1,0:T(8,128)(2,1)}, f32[256,1024]{1,0:T(8,128)}, bf16[256,1024]{1,0:T(8,128)(2,1)}, f32[256,128]{1,0:T(8,128)}, bf16[16,80,512]...) custom-call(bf16[16,128,128]{2,1,0:T(8,128)(2,1)} %get-tuple-element.58.recv_ref, ...), custom_call_target="tpu_custom_call" | custom-call | tf_op jit(solution)/shard_map/pallas_call | solution.py:49
  202.8 0.9 fusion.3.place_t_ref
  203.7 23.2 %shard_map.258 = (bf16[256,1024]{1,0:T(8,128)(2,1)}, f32[256,1024]{1,0:T(8,128)}, bf16[256,1024]{1,0:T(8,128)(2,1)}, bf16[16,128,128]{2,1,0:T(8,128)(2,1)}, f32[1024,128]{1,0:T(8,128)}, /*index=5*/f32[8,1024]{1,0:T(8,128)}) custom-call(bf16[16,80,512]{2,1,0:T(8,128)(2,1)} %get-tuple-element.64.out_ref, bf16[16,80,512]{2,1,0:T(8,128)(2,1)} %get-tuple-element.65.row_ref, ...), custom_call_target="tpu_custom_call" | custom-call | tf_op jit(solution)/shard_map/pallas_call | solution.py:49
  226.9 41.1 %shard_map.259 = (bf16[16,384,128]{2,1,0:T(8,128)(2,1)}, f32[8,128]{1,0:T(8,128)}) custom-call(s32[2,3]{1,0:T(2,128)} %bitcast.59, f32[8,128]{1,0:T(8,128)} %get-tuple-element.55.tab_ref, bf16[16,384,128]{2,1,0:T(8,128)(2,1)} %get-tuple-element.56.recv_ref, bf16[16,128,128]{2,1,0:T(8,128)(2,1)} %get-tuple-element.70.dout_ref, ...), custom_call_target="tpu_custom_call" | custom-call | tf_op jit(solution)/shard_map/pallas_call | solution.py:49
  268.0 52.2 %shard_map.260 = (bf16[256,1024]{1,0:T(8,128)(2,1)}, f32[48,1024]{1,0:T(8,128)}) custom-call(bf16[16,384,128]{2,1,0:T(8,128)(2,1)} %get-tuple-element.72.recv_ref, bf16[256,1024]{1,0:T(8,128)(2,1)} %get-tuple-element.73.normed_ref, bf16[256,1024]{1,0:T(8,128)(2,1)} %bitcast.47, f32[8,1024]{1,0:T(8,128)} %get-tuple-element.60.gain_ref.gains_ref, ...), custom_call_target="tpu_custom_call" | custom-call | tf_op jit(solution)/shard_map/pallas_call | solution.py:49
  320.2 3.9 %shard_map.261 = (f32[352,1024]{1,0:T(8,128)}, f32[352,1024]{1,0:T(8,128)}, f32[352,1024]{1,0:T(8,128)}, f32[8,1024]{1,0:T(8,128)}, f32[8,1024]{1,0:T(8,128)}, /...) custom-call(bf16[1056,1024]{1,0:T(8,128)(2,1)} %reduce-scatter.2.clo, ...), custom_call_target="tpu_custom_call" | custom-call | tf_op jit(solution)/shard_map/pallas_call | solution.py:49
  324.1 0.8 copy.44
  324.9 0.8 copy.45
  (28 shorter events, 0.2 us)
Async XLA Ops:
  7.2 117.8 %all-gather.3.cloned.1.call-start = ((), (), s32[]{:S(2)}) async-start(), calls=%async_computation.2 | async-start | bytes 19464192 | tf_op jit(solution)/shard_map/all_gather | solution.py:1005
  10.4 0.7 copy-start.2
  10.4 1.1 copy-start.3
  10.4 1.6 copy-start.4
  10.4 1.6 copy-start.5
  10.4 1.6 copy-start.6
  10.4 1.7 copy-start.7
  10.4 309.8 %reduce-scatter.2.cloned.1.call-start = ((), (), s32[]{:S(2)}) async-start(), calls=%async_computation.1 | async-start | bytes 19464192 | tf_op jit(solution)/shard_map/reduce_scatter | solution.py:1084
  320.2 3.9 %copy-start = (bf16[256,1024]{1,0:T(8,128)(2,1)S(1)}, bf16[256,1024]{1,0:T(8,128)(2,1)}, u32[]{:S(2)}) copy-start(bf16[256,1024]{1,0:T(8,128)(2,1)} %get-tuple-element.69) | copy-start | bytes 1572868
  320.2 4.7 %copy-start.1 = (bf16[256,1024]{1,0:T(8,128)(2,1)S(1)}, bf16[256,1024]{1,0:T(8,128)(2,1)}, u32[]{:S(2)}) copy-start(bf16[256,1024]{1,0:T(8,128)(2,1)} %get-tuple-element.83) | copy-start | bytes 1572868
Sparse Core Ops, SparseCore 0:
  10.6 91.2 all-gather.2
  202.9 103.5 reduce-scatter.1

commit v2 on v1

--- a/solution.py
+++ b/solution.py
@@ -25,7 +25,7 @@
 GELU_C = 0.7978845608028654
 BF = jnp.bfloat16
 F32 = jnp.float32
-VMEM_LIMIT = 58 * 1024 * 1024
+VMEM_LIMIT = 60 * 1024 * 1024
 
 
 def nn(left, right):
@@ -83,9 +83,8 @@
 GATHER_PARTS = ((pl.ds(0, 896), "xzy"), (pl.ds(896, 768), "xyz"))
 LATE_PARTS = ((pl.ds(OUT, 256), "xzy"), (pl.ds(OUT + 256, 256), "xyz"))
 REDUCE_PARTS = (
-    (pl.ds(0, 1024), "zyx"), (pl.ds(1024, 640), "yzx"), (pl.ds(1664, 384), "xyz"), (pl.ds(2048, 128), "yzx"),
+    (pl.ds(0, 1024), "zyx"), (pl.ds(1024, 768), "yzx"), (pl.ds(1792, 256), "xyz"), (pl.ds(2048, 128), "yzx"),
 )
-EARLY = 32
 MAIN = pl.ds(0, 4 * HALF)
 REST = pl.ds(4 * HALF, 128)
 
@@ -363,12 +362,11 @@
     return jnp.sum(jnp.where(at == row, values, 0.0), axis=-2)
 
 
-def gather_kernel(
-    x_ref, wq_ref, wk_ref, wv_ref, wo_ref, small_ref, place_ref, dy_ref,
-    normed_ref, land_ref, dy_land, dy_rest, wq_out, wk_out, wv_out, wo_out, wr_out, gain_out, tab_out,
-    box, out_ref, dy_hold, send_sem, recv_sem, *sems,
+def gather_part(
+    place, x_ref, wq_ref, wk_ref, wv_ref, wo_ref, small_ref, place_ref, dy_ref,
+    normed_ref, land_ref, dy_land, wq_out, wk_out, wv_out, wr_out, gain_out, tab_out,
+    box, out_ref, dy_hold, send_sem, recv_sem, sems,
 ):
-    place = Place()
     z, y, x, c = place.z, place.y, place.x, place.c
     for at, w_ref in ((0, wq_ref), (HALF, wk_ref), (2 * HALF, wv_ref), (OUT, wo_ref)):
         box[z, y, x, c, :, at : at + HALF] = folded(w_ref[...].astype(F32)).astype(BF)
@@ -397,25 +395,17 @@
         part.start_relay(2)
     for part in both:
         part.forward_all(1)
-    dy_rows = spread(nn(place_ref[...], dy_ref[...]))
-    dy_hold[...] = dy_rows[:, :EARLY]
-    dy_rest[...] = dy_rows[:, EARLY:]
+    dy_hold[...] = spread(nn(place_ref[...], dy_ref[...]))
     for part in both:
         part.arrive_relay(2)
     for part in late:
         part.arrive(0, forward=True)
         part.start(1)
-    early.start()
     for part in both:
         part.finish()
 
-    def unfold(at, w_out):
-        for plane in range(4):
-            value = box[plane, :, :, :, :, at : at + HALF].reshape(32, 16, HALF)
-            unfold_into(w_out, plane, value.astype(F32))
-
     for k, w_out in enumerate((wq_out, wk_out, wv_out)):
-        unfold(k * HALF, w_out)
+        unfold(box, k * HALF, w_out)
     small = box[:, :, :, :, :, SMALL:OUT].reshape(128, 16, 128).astype(F32)
     lane = lax.broadcasted_iota(jnp.int32, (D, 128), 1)
     wr_out[...] = jnp.where(lane < EXPERTS, small[:, :8, :].reshape(D, 128), 0.0).astype(BF)
@@ -449,19 +439,17 @@
                 trade.copy(part * 4 + ring(y, j)).start()
             else:
                 trade.keep()
-    for part in late:
-        part.arrive(2, forward=True)
-    for part in late:
-        part.finish()
-    unfold(OUT, wo_out)
-    trade.arrive()
-    early.arrive()
-    trade.drain()
-    early.drain()
-    copies.drain()
-
-
-def attn_setup(len_ref, tab_ref, recv_ref, kext, qext, bias):
+    early.start()
+    return copies, trade, early, late
+
+
+def unfold(box, at, w_out):
+    for plane in range(4):
+        value = box[plane, :, :, :, :, at : at + HALF].reshape(32, 16, HALF)
+        unfold_into(w_out, plane, value.astype(F32))
+
+
+def attn_setup(len_ref, recv_ref, kext, qext):
     rows = lax.broadcasted_iota(jnp.int32, (SEQ, 128), 0)
     lanes = lax.broadcasted_iota(jnp.int32, (SEQ, 128), 1)
     end1 = [len_ref[m, 0] for m in range(2)]
@@ -485,6 +473,10 @@
             feat = jnp.where((lane_in == 2 * m) & (pos >= end1[m]), MASKED, 0.0)
             feat = jnp.where((lane_in == 2 * m + 1) & (pos >= end2[m]), MASKED, feat)
             qext[i, m * TS : (m + 1) * TS, 128:] = feat.astype(BF)
+
+def bias_setup(tab_ref, bias):
+    row_in = lax.broadcasted_iota(jnp.int32, (TS, 128), 0)
+    lane_in = lax.broadcasted_iota(jnp.int32, (TS, 128), 1)
     for block in range(12):
         dist = 1024 - block * TS + lane_in - row_in
         if block in (7, 8):
@@ -525,14 +517,9 @@
     return pl.ds(pl.multiple_of(block * TS, TS), count * TS)
 
 
-def attn_fwd_kernel(
-    len_ref, tab_ref, recv_ref, dy_ref, land_ref, lse_ref, dy_land, kext, qext, bias, vt, out_ref, *sems
-):
-    greet(plane_peers())
+def attn_fwd_part(len_ref, recv_ref, land_ref, lse_ref, kext, qext, bias, vt, out_ref, sems):
     trade = Exchange(out_ref, land_ref, sems[0], sems[1])
-    early = Exchange(dy_ref, dy_land, sems[2], sems[3])
-    early.start()
-    attn_setup(len_ref, tab_ref, recv_ref, kext, qext, bias)
+    attn_setup(len_ref, recv_ref, kext, qext)
     unit = eye(TS)
     for i in range(EXPERTS):
         vt[:, i * TS : (i + 1) * TS] = nt(unit, recv_ref[i, 2 * TS : 3 * TS, :]).astype(BF)
@@ -552,20 +539,42 @@
         trade.push(i)
 
     strips(strip, after)
+    return trade
+
+
+def head_kernel(
+    len_ref, x_ref, wq_ref, wk_ref, wv_ref, wo_ref, small_ref, place_ref, dy_ref,
+    normed_ref, heads_ref, dy_land, wq_out, wk_out, wv_out, wo_out, wr_out, gain_out, tab_out, att_land, lse_ref,
+    box, head_hold, dy_hold, kext, qext, bias, vt, att_hold, send_sem, recv_sem, *sems,
+):
+    copies, trade, early, late = gather_part(
+        Place(), x_ref, wq_ref, wk_ref, wv_ref, wo_ref, small_ref, place_ref, dy_ref,
+        normed_ref, heads_ref, dy_land, wq_out, wk_out, wv_out, wr_out, gain_out, tab_out,
+        box, head_hold, dy_hold, send_sem, recv_sem, sems[0:4],
+    )
+    bias_setup(tab_out, bias)
     trade.arrive()
-    early.arrive()
-    trade.drain()
-    early.drain()
-
-
-def attn_bwd_kernel(
+    for part in late:
+        part.arrive(2, forward=True)
+    back = attn_fwd_part(len_ref, heads_ref, att_land, lse_ref, kext, qext, bias, vt, att_hold, sems[4:6])
+    for part in late:
+        part.finish()
+    unfold(box, OUT, wo_out)
+    for sent in (back, early):
+        sent.arrive()
+    for sent in (trade, back, early):
+        sent.drain()
+    copies.drain()
+
+
+def attn_bwd_part(
     len_ref, tab_ref, recv_ref, dout_ref, lse_ref, land_ref, tab_out_ref,
-    kext, qext, bias, ktext, dk, dv, near, far, out_ref, *sems,
+    kext, qext, bias, ktext, dk, dv, near, far, out_ref, sems, ready, meanwhile,
 ):
-    greet(plane_peers())
     trade_q = Exchange(out_ref, land_ref, sems[0], sems[1], pl.ds(0, TS))
     trade_kv = Exchange(out_ref, land_ref, sems[2], sems[3], pl.ds(TS, 2 * TS))
-    attn_setup(len_ref, tab_ref, recv_ref, kext, qext, bias)
+    attn_setup(len_ref, recv_ref, kext, qext)
+    bias_setup(tab_ref, bias)
     unit = eye(256)
     for i in range(EXPERTS):
         ktext[:, i * TS : (i + 1) * TS] = nt(unit, kext[i * TS : (i + 1) * TS, :])[:144].astype(BF)
@@ -608,6 +617,8 @@
         out_ref[i, 2 * TS :, :] = dv[span(i, 1), :].astype(BF)
         trade_kv.push(i)
 
+    ready()
+
     odd = lax.rem(trade_kv.me, 2)
 
     def first_half(low, count):
@@ -658,9 +669,10 @@
         res = jnp.where(lane == b, part, res)
     res = jnp.where(lane == NB - 1, total - seen, res)
     tab_out_ref[...] = res
+    meanwhile()
     for trade in (trade_q, trade_kv):
         trade.arrive()
-        trade.drain()
+    return trade_q, trade_kv
 
 
 def row_expert():
@@ -698,7 +710,7 @@
 
 
 def moe_kernel(
-    recv_ref, x_ref, wo_ref, gain_ref, wr_ref, mask_ref, place_ref, dy_ref, dy_late_ref, w_ref,
+    recv_ref, x_ref, wo_ref, gain_ref, wr_ref, mask_ref, place_ref, dy_ref, w_ref,
     att_ref, hidden_ref, mixed_ref, share_ref, back_out, back_row, grads_ref,
     w_buf, hold_a, hold_b, land_a, hold_s, land_s, rows, slots, act, first, second, acc, stage,
     w_sem, stage_sem, *sems,
@@ -748,7 +760,7 @@
     hold_s[...] = jnp.concatenate([value, jnp.zeros((EXPERTS, 8, 128), F32)], axis=1).astype(BF)
     to_shares.start()
 
-    unspread(slots, dy_ref, dy_late_ref)
+    unspread(slots, dy_ref)
     for copy in loads[2]:
         copy.wait()
     for at, size in CHUNKS:
@@ -819,12 +831,11 @@
     to_shares.drain()
 
 
-def back_kernel(
+def back_part(
     out_ref, row_ref, place_ref, place_t_ref, dy_ref, hidden_ref, mixed_ref, share_ref, wr_ref, gain_ref, wo_ref,
     result_ref, hgrad_ref, branch_ref, land_ref, router_ref, gain_out_ref,
     send_ref, outs, rows, send_sem, recv_sem,
 ):
-    greet(plane_peers())
     z, y, _, _ = coords()
     trade = Exchange(send_ref, land_ref, send_sem, recv_sem)
     unspread(outs, out_ref)
@@ -876,19 +887,15 @@
     router_ref[...] = tn(mixed, lg_high) + tn(mixed, lg_low)
     moe = nn(scale_high, returned) + nn(scale_low, returned)
     result_ref[...] = (hidden + moe).astype(BF)
-    trade.arrive()
-    trade.drain()
-
-
-def final_kernel(
-    recv_ref, normed_ref, x_ref, gains_ref, hgrad_ref, wq_ref, wk_ref, wv_ref,
-    att_ref, branch_ref, router_ref, moe_gain_ref, table_ref, igrad_ref, sum_ref,
-    flat_q, flat_k, flat_v, box, from_twin, *rest,
+    return trade
+
+
+def final_part(
+    place, copies, recv_ref, normed_ref, x_ref, gains_ref, hgrad_ref, wq_ref, wk_ref, wv_ref,
+    router_ref, moe_gain_ref, table_ref, igrad_ref, sum_ref,
+    flat_q, flat_k, flat_v, box, from_twin, rest,
 ):
-    place = Place()
     z, y, c = place.z, place.y, place.c
-    greet(place.peers("xyz") + [place.twin])
-    copies = Copies(rest[20], rest[21])
     parts = [
         Reduce(
             place, copies, order, (from_twin, lanes),
@@ -917,12 +924,8 @@
             parts[0].send(0, k + 1)
 
     for k, plane in enumerate(planes):
-        cols = pl.ds(pl.multiple_of(plane * 256, 256), 256)
-        for which, (left, flat) in enumerate(
-            ((normed_ref, flat_q), (normed_ref, flat_k), (normed_ref, flat_v), (att_ref, branch_ref))
-        ):
-            value = fold_rows(tn(left[:, cols], flat[...])).astype(BF)
-            box[plane, :, :, :, :, which * HALF : (which + 1) * HALF] = value.reshape(4, 4, 2, 16, HALF)
+        for which, flat in enumerate(flats):
+            plane_grads(box, plane, which, normed_ref, flat)
         to_twin.append(
             copies.go(
                 box.at[plane, :, :, 1 - c, :, MAIN], from_twin.at[plane, :, :, :, MAIN], place.twin
@@ -968,6 +971,45 @@
     for which in range(4):
         sum_ref[which * 8 : which * 8 + 8, :] = unfolded(value[:, which * HALF : (which + 1) * HALF])
     sum_ref[32:48, 0:128] = value[:, 4 * HALF :]
+
+
+def plane_grads(box, plane, which, left, right):
+    cols = pl.ds(pl.multiple_of(plane * 256, 256), 256)
+    value = fold_rows(tn(left[:, cols], right[...])).astype(BF)
+    box[plane, :, :, :, :, which * HALF : (which + 1) * HALF] = value.reshape(4, 4, 2, 16, HALF)
+
+
+def tail_kernel(
+    len_ref, tab_ref, out_ref, row_ref, place_ref, place_t_ref, dy_ref, hidden_ref, mixed_ref, share_ref,
+    wr_ref, gains_ref, wo_ref, heads_ref, lse_ref, normed_ref, x_ref, wq_ref, wk_ref, wv_ref, att_ref,
+    result_ref, igrad_ref, sum_ref,
+    hgrad, branch, head_grads, router, moe_gain, head_send, outs, rows,
+    kext, qext, bias, ktext, dk, dv, near, far, grads_send, token_grads, table,
+    flat_q, flat_k, flat_v, box, from_twin, *rest,
+):
+    place = Place()
+    greet(plane_peers() + place.peers("x") + [place.twin])
+    copies = Copies(rest[20], rest[21])
+    sems = rest[22:]
+    trade = back_part(
+        out_ref, row_ref, place_ref, place_t_ref, dy_ref, hidden_ref, mixed_ref, share_ref, wr_ref, gains_ref,
+        wo_ref, result_ref, hgrad, branch, head_grads, router, moe_gain, head_send, outs, rows, sems[0], sems[1],
+    )
+
+    def out_grads():
+        for plane in range(4):
+            plane_grads(box, plane, 3, att_ref, branch)
+
+    trades = attn_bwd_part(
+        len_ref, tab_ref, heads_ref, head_grads, lse_ref, token_grads, table,
+        kext, qext, bias, ktext, dk, dv, near, far, grads_send, sems[2:6], trade.arrive, out_grads,
+    )
+    final_part(
+        place, copies, token_grads, normed_ref, x_ref, gains_ref, hgrad, wq_ref, wk_ref, wv_ref,
+        router, moe_gain, table, igrad_ref, sum_ref, flat_q, flat_k, flat_v, box, from_twin, rest,
+    )
+    for sent in (trade,) + trades:
+        sent.drain()
     copies.drain()
 
 
@@ -1023,40 +1065,30 @@
     lengths = doc_lengths[:, 0]
 
     chunk = (EXPERTS, 4 * CAP, HALF)
-    early, rest = (EXPERTS, EARLY, HALF), (EXPERTS, 4 * CAP - EARLY, HALF)
-    normed, heads, dy_early, dy_rest, wq, wk, wv, wo, wr, gains, table = call(
-        gather_kernel,
-        (
-            shape((TOK, D), BF), shape((H, 3 * TS, 128), BF), shape(early, BF), shape(rest, BF), shape((D, D), BF), shape((D, D), BF),
-            shape((D, D), BF), shape((D, D), BF), shape((D, 128), BF), shape((8, D), F32), shape((8, 128), F32),
-        ),
-        x, w_query, w_key, w_value, w_out, small, place, dy,
-        scratch=[
-            pltpu.VMEM((4, 4, 4, 2, 16, WIDE), BF),
-            pltpu.VMEM((H, 3 * TS, 128), BF),
-            pltpu.VMEM(early, BF),
-            pltpu.SemaphoreType.DMA((78,)),
-            pltpu.SemaphoreType.DMA((78,)),
-        ]
-        + [pltpu.SemaphoreType.DMA((EXPERTS,))] * 4,
-        collective_id=1,
-    )
+    chunk = (EXPERTS, 4 * CAP, HALF)
     smem = pl.BlockSpec(memory_space=pltpu.SMEM)
     vmem = pl.BlockSpec(memory_space=pltpu.VMEM)
     attn_scratch = [
-        pltpu.VMEM((SEQ, 256), BF),
-        pltpu.VMEM((EXPERTS, TOK, 256), BF),
-        pltpu.VMEM((12 * TS, TOK), F32),
+        pltpu.VMEM((SEQ, 256), BF), pltpu.VMEM((EXPERTS, TOK, 256), BF), pltpu.VMEM((12 * TS, TOK), F32),
     ]
-    att_back, lse, dy_late = call(
-        attn_fwd_kernel,
-        (shape((EXPERTS, TS, 128), BF), shape((EXPERTS, 8, TOK), F32), shape(rest, BF)),
-        lengths, table, heads, dy_rest,
-        in_specs=[smem] + [vmem] * 3,
-        scratch=attn_scratch
+    matrix = shape((D, D), BF)
+    normed, heads, dy_rows, wq, wk, wv, wo, wr, gains, table, att_back, lse = call(
+        head_kernel,
+        (
+            shape((TOK, D), BF), shape((H, 3 * TS, 128), BF), shape(chunk, BF), matrix, matrix, matrix, matrix,
+            shape((D, 128), BF), shape((8, D), F32), shape((8, 128), F32),
+            shape((EXPERTS, TS, 128), BF), shape((EXPERTS, 8, TOK), F32),
+        ),
+        lengths, x, w_query, w_key, w_value, w_out, small, place, dy,
+        in_specs=[smem] + [vmem] * 8,
+        scratch=[
+            pltpu.VMEM((4, 4, 4, 2, 16, WIDE), BF), pltpu.VMEM((H, 3 * TS, 128), BF), pltpu.VMEM(chunk, BF),
+        ]
+        + attn_scratch
         + [pltpu.VMEM((128, SEQ), BF), pltpu.VMEM((EXPERTS, TS, 128), BF)]
-        + [pltpu.SemaphoreType.DMA((EXPERTS,))] * 4,
-        collective_id=5,
+        + [pltpu.SemaphoreType.DMA((78,))] * 2
+        + [pltpu.SemaphoreType.DMA((EXPERTS,))] * 6,
+        collective_id=1,
     )
     anywhere = pl.BlockSpec(memory_space=pl.ANY)
     att, hidden, mixed, share, outs, row_grads, expert_grads = call(
@@ -1065,8 +1097,8 @@
             shape((TOK, D), BF), shape((TOK, D), F32), shape((TOK, D), BF), shape((TOK, 128), F32),
             shape(chunk, BF), shape(chunk, BF), shape((FSDP, 3 * SHARD, D), BF),
         ),
-        att_back, x, wo, gains, wr, picked, place, dy_early, dy_late, expert_w,
-        in_specs=[vmem] * 9 + [anywhere],
+        att_back, x, wo, gains, wr, picked, place, dy_rows, expert_w,
+        in_specs=[vmem] * 8 + [anywhere],
         out_specs=(vmem,) * 6 + (anywhere,),
         scratch=[
             pltpu.VMEM((3, FF, D), BF),
@@ -1084,47 +1116,30 @@
     expert_sum = lax.psum_scatter(
         expert_grads.reshape(FSDP * 3 * SHARD, D), "fsdp", scatter_dimension=0, tiled=True
     )
-    result, hgrad, branch, head_grads, router_grad, moe_gain_grad = call(
-        back_kernel,
-        (
-            shape((TOK, D), BF), shape((TOK, D), F32), shape((TOK, D), BF),
-            shape((H, TS, 128), BF), shape((D, 128), F32), shape((8, D), F32),
-        ),
-        outs, row_grads, place, place_t, dy, hidden, mixed, share, wr, gains, wo,
+    result, input_grad, sums = call(
+        tail_kernel,
+        (shape((TOK, D), BF), shape((TOK, D), BF), shape((48, D), F32)),
+        lengths, table, outs, row_grads, place, place_t, dy, hidden, mixed, share, wr, gains, wo,
+        heads, lse, normed, x, wq, wk, wv, att,
+        in_specs=[smem] + [vmem] * 20,
         scratch=[
-            pltpu.VMEM((H, TS, 128), BF), pltpu.VMEM((BUF, D), BF), pltpu.VMEM((BUF, D), BF),
-            pltpu.SemaphoreType.DMA((EXPERTS,)), pltpu.SemaphoreType.DMA((EXPERTS,)),
-        ],
-        collective_id=4,
-    )
-    token_grads, table_grad = call(
-        attn_bwd_kernel,
-        (shape((EXPERTS, 3 * TS, 128), BF), shape((8, 128), F32)),
-        lengths, table, heads, head_grads, lse,
-        in_specs=[smem] + [vmem] * 4,
-        scratch=attn_scratch
+            pltpu.VMEM((TOK, D), F32), pltpu.VMEM((TOK, D), BF), pltpu.VMEM((H, TS, 128), BF),
+            pltpu.VMEM((D, 128), F32), pltpu.VMEM((8, D), F32), pltpu.VMEM((H, TS, 128), BF),
+            pltpu.VMEM((BUF, D), BF), pltpu.VMEM((BUF, D), BF),
+        ]
+        + attn_scratch
         + [
-            pltpu.VMEM((144, SEQ), BF),
-            pltpu.VMEM((SEQ, 128), F32),
-            pltpu.VMEM((SEQ, 128), F32),
-            pltpu.VMEM((2 * TS, TOK), F32),
-            pltpu.VMEM((8, TOK), F32),
-            pltpu.VMEM((EXPERTS, 3 * TS, 128), BF),
-        ]
-        + [pltpu.SemaphoreType.DMA((EXPERTS,))] * 4,
-        collective_id=6,
-    )
-    input_grad, sums = call(
-        final_kernel,
-        (shape((TOK, D), BF), shape((48, D), F32)),
-        token_grads, normed, x, gains, hgrad, wq, wk, wv, att, branch, router_grad, moe_gain_grad, table_grad,
-        scratch=[
+            pltpu.VMEM((144, SEQ), BF), pltpu.VMEM((SEQ, 128), F32), pltpu.VMEM((SEQ, 128), F32),
+            pltpu.VMEM((2 * TS, TOK), F32), pltpu.VMEM((8, TOK), F32),
+            pltpu.VMEM((EXPERTS, 3 * TS, 128), BF), pltpu.VMEM((EXPERTS, 3 * TS, 128), BF),
+            pltpu.VMEM((8, 128), F32),
             pltpu.VMEM((TOK, D), BF), pltpu.VMEM((TOK, D), BF), pltpu.VMEM((TOK, D), BF),
             pltpu.VMEM((4, 4, 4, 2, 16, WIDE), BF),
             pltpu.VMEM((4, 4, 4, 16, WIDE), BF),
         ]
         + [buf for lanes, _ in REDUCE_PARTS for buf in reduce_scratch(lanes.size)]
-        + [pltpu.SemaphoreType.DMA((41,))] * 2,
+        + [pltpu.SemaphoreType.DMA((41,))] * 2
+        + [pltpu.SemaphoreType.DMA((EXPERTS,))] * 6,
         collective_id=2,
     )
     block = shape((SHARD, D), F32)

time: 336 us -> 311 us (0.926)
  Pallas kernels: 308 us -> 281 us
    pallas_call x7 -> x4, Pallas kernels: 308 us -> 281 us  [call(): pl.pallas_call(kernel, out_shape=out_shape, in_specs=in_specs or [pl.Bloc...]
  transfers between devices with their start and end apart: 2 -> 2, of which waited for: 0 -> 1; matrix products, arithmetic and copies ran while one was open for 2% -> 2% of each run, Pallas kernels for 68% -> 69%
where the time goes in v2:
time: 311 us; the launch traced here: 306 us
  Pallas kernels  281 us (90%)
  between operations  14.7 us (5%)
  other arithmetic  6.11 us (2%)
  local copies, waits for them, and re-layouts  4.25 us (1%)
    pallas_call x4, Pallas kernels, call(): pl.pallas_call(kernel, out_shape=out_shape, in_specs=in_specs or [pl.Bloc...  281 us
  transfers between devices with their start and end apart: 2, of which 1 were waited for; matrix products, arithmetic and copies ran while one was open for 2% of the time, Pallas kernels for 69%

profile of v2, /device:TPU:1, one launch (start us, length us, event | category | flops | bytes accessed | tf_op | source)
XLA Modules:
  0.0 306.2 jit_solution(12052828153352789787)
XLA Ops:
  7.2 0.0 all-gather.3.cloned.1.call-start
  7.2 3.1 %pad_maximum_fusion = bf16[1056,1024]{1,0:T(8,128)(2,1)} fusion(bf16[352,1024]{1,0:T(8,128)(2,1)} %bitcast.50, bf16[352,1024]{1,0:T(8,128)(2,1)} %bitcast.51, bf16[352,1024]{1,0:T(8,128)(2,1)} %bitcast.52), kind=kLoop, calls=%fused_computation | loop fusion | flops 6488064 | bytes 4325376 | tf_op jit(solution)/shard_map/concatenate | solution.py:1046
  10.4 0.0 all-gather.3.cloned.1.call-update
  10.4 0.0 reduce-scatter.2.cloned.1.call-start
  10.5 0.6 copy-done.2
  11.1 0.1 copy.35
  11.2 0.1 copy.36
  11.3 0.1 eq.102
  11.5 0.3 convert_reduce_fusion
  11.8 0.1 reduce_sum.12
  12.1 1.2 concatenate.6.small_ref
  13.3 0.1 broadcast_bitcast_fusion
  13.3 0.1 add_select_fusion
  13.5 0.2 slice_reduce_fusion.1
  13.7 0.9 fusion.1.place_ref
  14.5 102.3 %shard_map.255 = (bf16[256,1024]{1,0:T(8,128)(2,1)}, bf16[16,384,128]{2,1,0:T(8,128)(2,1)}, bf16[16,80,512]{2,1,0:T(8,128)(2,1)}, bf16[1024,1024]{1,0:T(8,128)(2...) custom-call(s32[2,3]{1,0:T(2,128)} %bitcast.58, ...), custom_call_target="tpu_custom_call" | custom-call | tf_op jit(solution)/shard_map/pallas_call | solution.py:49
  116.8 0.8 fusion.5.mask_ref
  117.6 66.9 %shard_map.256 = (bf16[256,1024]{1,0:T(8,128)(2,1)}, f32[256,1024]{1,0:T(8,128)}, bf16[256,1024]{1,0:T(8,128)(2,1)}, f32[256,128]{1,0:T(8,128)}, bf16[16,80,512]...) custom-call(bf16[16,128,128]{2,1,0:T(8,128)(2,1)} %get-tuple-element.47.recv_ref, ...), custom_call_target="tpu_custom_call" | custom-call | tf_op jit(solution)/shard_map/pallas_call | solution.py:49
  184.5 0.9 fusion.3.place_t_ref
  185.4 107.6 %shard_map.257 = (bf16[256,1024]{1,0:T(8,128)(2,1)}, bf16[256,1024]{1,0:T(8,128)(2,1)}, f32[48,1024]{1,0:T(8,128)}) custom-call(s32[2,3]{1,0:T(2,128)} %bitcast.59, f32[8,128]{1,0:T(8,128)} %get-tuple-element.46.tab_ref, bf16[16,80,512]{2,1,0:T(8,128)(2,1)} %get-tuple-element.52.out_ref, bf16[16,80,512]{2,1,0:T(8,128)(2,1)} %get-tuple-element.53.row_ref, ...), custom_call_target="tpu_custom_call" | custom-call | tf_op jit(solution)/shard_map/pallas_call | solution.py:49
  293.0 0.5 reduce-scatter.2.cloned.1.call-done.expert_ref
  293.5 3.8 %shard_map.258 = (f32[352,1024]{1,0:T(8,128)}, f32[352,1024]{1,0:T(8,128)}, f32[352,1024]{1,0:T(8,128)}, f32[8,1024]{1,0:T(8,128)}, f32[8,1024]{1,0:T(8,128)}, /...) custom-call(bf16[1056,1024]{1,0:T(8,128)(2,1)} %reduce-scatter.2.clo, ...), custom_call_target="tpu_custom_call" | custom-call | tf_op jit(solution)/shard_map/pallas_call | solution.py:49
  297.4 0.8 copy.44
  298.2 0.8 copy.45
  (25 shorter events, 0.1 us)
Async XLA Ops:
  7.2 110.4 %all-gather.3.cloned.1.call-start = ((), (), s32[]{:S(2)}) async-start(), calls=%async_computation.2 | async-start | bytes 19464192 | tf_op jit(solution)/shard_map/all_gather | solution.py:1047
  10.4 0.7 copy-start.2
  10.4 1.1 copy-start.3
  10.4 1.6 copy-start.4
  10.4 1.6 copy-start.5
  10.4 1.6 copy-start.6
  10.4 1.7 copy-start.7
  10.4 283.1 %reduce-scatter.2.cloned.1.call-start = ((), (), s32[]{:S(2)}) async-start(), calls=%async_computation.1 | async-start | bytes 19464192 | tf_op jit(solution)/shard_map/reduce_scatter | solution.py:1116
  293.0 4.3 %copy-start.1 = (bf16[256,1024]{1,0:T(8,128)(2,1)S(1)}, bf16[256,1024]{1,0:T(8,128)(2,1)}, u32[]{:S(2)}) copy-start(bf16[256,1024]{1,0:T(8,128)(2,1)} %get-tuple-element.64) | copy-start | bytes 1572868
  293.0 5.1 %copy-start = (bf16[256,1024]{1,0:T(8,128)(2,1)S(1)}, bf16[256,1024]{1,0:T(8,128)(2,1)}, u32[]{:S(2)}) copy-start(bf16[256,1024]{1,0:T(8,128)(2,1)} %get-tuple-element.65) | copy-start | bytes 1572868
Sparse Core Ops, SparseCore 0:
  10.6 91.2 all-gather.2
  184.6 108.8 reduce-scatter.1

commit v3 on v2

--- a/solution.py
+++ b/solution.py
@@ -83,7 +83,7 @@
 GATHER_PARTS = ((pl.ds(0, 896), "xzy"), (pl.ds(896, 768), "xyz"))
 LATE_PARTS = ((pl.ds(OUT, 256), "xzy"), (pl.ds(OUT + 256, 256), "xyz"))
 REDUCE_PARTS = (
-    (pl.ds(0, 1024), "zyx"), (pl.ds(1024, 768), "yzx"), (pl.ds(1792, 256), "xyz"), (pl.ds(2048, 128), "yzx"),
+    (pl.ds(0, 1152), "zyx"), (pl.ds(1152, 640), "yzx"), (pl.ds(1792, 256), "xyz"), (pl.ds(2048, 128), "yzx"),
 )
 MAIN = pl.ds(0, 4 * HALF)
 REST = pl.ds(4 * HALF, 128)
@@ -1015,7 +1015,7 @@
 
 def emit_kernel(expert_ref, sum_ref, gate, up, down, gq, gk, gv, go, router, gain_attn, gain_moe, table):
     for k, ref in enumerate((gate, up, down)):
-        ref[...] = expert_ref[k * SHARD : (k + 1) * SHARD, :].astype(F32)
+        ref[...] = expert_ref[k].astype(F32)
     for k, ref in enumerate((gq, gk, gv, go)):
         ref[...] = sum_ref[k * 8 : k * 8 + 8, :]
     router[...] = sum_ref[32:40, :EXPERTS]
@@ -1144,12 +1144,19 @@
     )
     block = shape((SHARD, D), F32)
     rows = shape((8, D), F32)
-    gate, up, down, gq, gk, gv, go, router, gain_a, gain_m, table_sum = call(
+    small_shapes = (rows, rows, rows, rows) + tuple(
+        shape(dims, F32) for dims in ((8, EXPERTS), (1, 8), (1, 8), (1, 4))
+    )
+    part = SHARD // 2
+    gate, up, down, gq, gk, gv, go, router, gain_a, gain_m, table_sum = pl.pallas_call(
         emit_kernel,
-        (block, block, block, rows, rows, rows, rows)
-        + tuple(shape(dims, F32) for dims in ((8, EXPERTS), (1, 8), (1, 8), (1, 4))),
-        expert_sum, sums,
-    )
+        grid=(2,),
+        out_shape=(block, block, block) + small_shapes,
+        in_specs=[pl.BlockSpec((3, part, D), lambda i: (0, i, 0)), pl.BlockSpec((48, D), lambda i: (0, 0))],
+        out_specs=(pl.BlockSpec((part, D), lambda i: (i, 0)),) * 3
+        + tuple(pl.BlockSpec(small_shape.shape, lambda i: (0, 0)) for small_shape in small_shapes),
+        compiler_params=pltpu.CompilerParams(vmem_limit_bytes=VMEM_LIMIT),
+    )(expert_sum.reshape(3, SHARD, D), sums)
     return (
         result.reshape(tokens.shape), input_grad.reshape(tokens.shape), gain_a[0], gq, gk, gv, go,
         table_sum[0], gain_m[0], router, gate.T[None], up.T[None], down[None],

time: 311 us -> 313 us (level)
    pallas_call x0 -> x1, Pallas kernels: none -> 3.56 us  [on_device(): pl.pallas_call(emit_kernel, grid=(2,), out_shape=(block, block, block) +...]
    pallas_call x4 -> x3, Pallas kernels: 281 us -> 280 us  [call(): pl.pallas_call(kernel, out_shape=out_shape, in_specs=in_specs or [pl.Bloc...]
  transfers between devices with their start and end apart: 2 -> 2, of which waited for: 1 -> 0; matrix products, arithmetic and copies ran while one was open for 2% -> 2% of each run, Pallas kernels for 69% -> 69%
where the time goes in v3:
time: 313 us; the launch traced here: 309 us
  Pallas kernels  284 us (91%)
  between operations  14.7 us (5%)
  other arithmetic  6.11 us (2%)
  local copies, waits for them, and re-layouts  4.25 us (1%)
    pallas_call x3, Pallas kernels, call(): pl.pallas_call(kernel, out_shape=out_shape, in_specs=in_specs or [pl.Bloc...  280 us
  transfers between devices with their start and end apart: 2, of which 0 were waited for; matrix products, arithmetic and copies ran while one was open for 2% of the time, Pallas kernels for 69%

profile of v3, /device:TPU:1, one launch (start us, length us, event | category | flops | bytes accessed | tf_op | source)
XLA Modules:
  0.0 308.7 jit_solution(387321386626022399)
XLA Ops:
  7.2 0.0 all-gather.3.cloned.1.call-start
  7.2 3.1 %pad_maximum_fusion = bf16[1056,1024]{1,0:T(8,128)(2,1)} fusion(bf16[352,1024]{1,0:T(8,128)(2,1)} %bitcast.52, bf16[352,1024]{1,0:T(8,128)(2,1)} %bitcast.53, bf16[352,1024]{1,0:T(8,128)(2,1)} %bitcast.54), kind=kLoop, calls=%fused_computation | loop fusion | flops 6488064 | bytes 4325376 | tf_op jit(solution)/shard_map/concatenate | solution.py:1046
  10.4 0.0 all-gather.3.cloned.1.call-update
  10.4 0.0 reduce-scatter.2.cloned.1.call-start
  10.5 0.6 copy-done.2
  11.1 0.1 copy.35
  11.2 0.1 copy.36
  11.3 0.1 eq.102
  11.5 0.3 convert_reduce_fusion
  11.8 0.1 reduce_sum.12
  12.1 1.2 concatenate.6.small_ref
  13.3 0.1 broadcast_bitcast_fusion
  13.3 0.1 add_select_fusion
  13.5 0.2 slice_reduce_fusion.1
  13.7 0.9 fusion.1.place_ref
  14.5 102.3 %shard_map.255 = (bf16[256,1024]{1,0:T(8,128)(2,1)}, bf16[16,384,128]{2,1,0:T(8,128)(2,1)}, bf16[16,80,512]{2,1,0:T(8,128)(2,1)}, bf16[1024,1024]{1,0:T(8,128)(2...) custom-call(s32[2,3]{1,0:T(2,128)} %bitcast.60, ...), custom_call_target="tpu_custom_call" | custom-call | tf_op jit(solution)/shard_map/pallas_call | solution.py:49
  116.8 0.8 fusion.5.mask_ref
  117.6 66.9 %shard_map.256 = (bf16[256,1024]{1,0:T(8,128)(2,1)}, f32[256,1024]{1,0:T(8,128)}, bf16[256,1024]{1,0:T(8,128)(2,1)}, f32[256,128]{1,0:T(8,128)}, bf16[16,80,512]...) custom-call(bf16[16,128,128]{2,1,0:T(8,128)(2,1)} %get-tuple-element.47.recv_ref, ...), custom_call_target="tpu_custom_call" | custom-call | tf_op jit(solution)/shard_map/pallas_call | solution.py:49
  184.5 0.9 fusion.3.place_t_ref
  185.4 110.8 %shard_map.257 = (bf16[256,1024]{1,0:T(8,128)(2,1)}, bf16[256,1024]{1,0:T(8,128)(2,1)}, f32[48,1024]{1,0:T(8,128)}) custom-call(s32[2,3]{1,0:T(2,128)} %bitcast.61, f32[8,128]{1,0:T(8,128)} %get-tuple-element.46.tab_ref, bf16[16,80,512]{2,1,0:T(8,128)(2,1)} %get-tuple-element.52.out_ref, bf16[16,80,512]{2,1,0:T(8,128)(2,1)} %get-tuple-element.53.row_ref, ...), custom_call_target="tpu_custom_call" | custom-call | tf_op jit(solution)/shard_map/pallas_call | solution.py:49
  296.2 0.0 reduce-scatter.2.cloned.1.call-done
  296.3 3.6 %shard_map.258 = (f32[352,1024]{1,0:T(8,128)}, f32[352,1024]{1,0:T(8,128)}, f32[352,1024]{1,0:T(8,128)}, f32[8,1024]{1,0:T(8,128)}, f32[8,1024]{1,0:T(8,128)}, /...) custom-call(bf16[3,352,1024]{2,1,0:T(8,128)(2,1)} %bitcast.49, ...), custom_call_target="tpu_custom_call" | custom-call | tf_op jit(solution)/shard_map/pallas_call | solution.py:1151
  299.8 0.8 copy.44
  300.6 0.8 copy.45
  (25 shorter events, 0.1 us)
Async XLA Ops:
  7.2 110.4 %all-gather.3.cloned.1.call-start = ((), (), s32[]{:S(2)}) async-start(), calls=%async_computation.2 | async-start | bytes 19464192 | tf_op jit(solution)/shard_map/all_gather | solution.py:1047
  10.4 0.7 copy-start.2
  10.4 1.1 copy-start.3
  10.4 1.6 copy-start.4
  10.4 1.6 copy-start.5
  10.4 1.6 copy-start.6
  10.4 1.7 copy-start.7
  10.4 285.8 %reduce-scatter.2.cloned.1.call-start = ((), (), s32[]{:S(2)}) async-start(), calls=%async_computation.1 | async-start | bytes 19464192 | tf_op jit(solution)/shard_map/reduce_scatter | solution.py:1116
  296.2 3.6 %copy-start.1 = (bf16[256,1024]{1,0:T(8,128)(2,1)S(1)}, bf16[256,1024]{1,0:T(8,128)(2,1)}, u32[]{:S(2)}) copy-start(bf16[256,1024]{1,0:T(8,128)(2,1)} %get-tuple-element.64) | copy-start | bytes 1572868
  296.2 4.4 %copy-start = (bf16[256,1024]{1,0:T(8,128)(2,1)S(1)}, bf16[256,1024]{1,0:T(8,128)(2,1)}, u32[]{:S(2)}) copy-start(bf16[256,1024]{1,0:T(8,128)(2,1)} %get-tuple-element.65) | copy-start | bytes 1572868
Sparse Core Ops, SparseCore 0:
  10.6 91.2 all-gather.2
  184.6 106.2 reduce-scatter.1
